TPU v7x, 512 devices: a whole 4x4x16 slice. The times are simulated.
512 devices in a mesh: lat: 8 (over y, core), lon: 32 (over x_lo, z), dp: 2 (over x_hi).
Axes of the slice: x: 4 (x_hi: 2, x_lo: 2; x = x_hi * 2 + x_lo), y: 4, z: 16, core: 2. Of those that a mesh axis runs over, the one named last changes fastest.
Arguments:
- field: bfloat16 [2, 2, 96, 192, 384], P('dp', None, 'lat', 'lon'), may hold values from -6 to 6
- cotangent: bfloat16 [2, 2, 96, 192, 384], P('dp', None, 'lat', 'lon'), may hold values from -6 to 6
- qkv_plain: bfloat16 [384, 1152], P(None, 'dp'), may hold values from -0.3125 to 0.3125
- proj_plain: bfloat16 [384, 384], replicated, may hold values from -0.3125 to 0.3125
- bias_plain: bfloat16 [1, 8, 12, 6336], P(None, 'lat'), may hold values from -4 to 264
- qkv_shift: bfloat16 [384, 1152], P(None, 'dp'), may hold values from -0.3125 to 0.3125
- proj_shift: bfloat16 [384, 384], replicated, may hold values from -0.3125 to 0.3125
- bias_shift: bfloat16 [1, 8, 12, 6336], P(None, 'lat'), may hold values from -4 to 264
Outputs:
- out_field: bfloat16 [2, 2, 96, 192, 384], P('dp', None, 'lat', 'lon')
- grad_field: bfloat16 [2, 2, 96, 192, 384], P('dp', None, 'lat', 'lon')
- grad_proj_plain: bfloat16 [384, 384], replicated
- grad_proj_shift: bfloat16 [384, 384], replicated
All inputs are finite; a program needn't handle non-finite values.
Results may differ from a plain program's by a relative error of at most 0.015.
Values may be sent and summed in bfloat16 or wider, within the bound.
A program may use at most 128 MiB of HBM per device.

v0:
```python
import jax
import jax.numpy as jnp
from jax import lax
from jax.sharding import PartitionSpec as P

HEADS = 12
LEV = 2
WLEV = 2
WLAT = 12
WLON = 6
LONW = 1


def shifted_2(x, axis, by):
    length = lax.axis_size(axis)
    return lax.ppermute(x, axis, [(i, (i + by) % length) for i in range(length)])


def expand_bias(table):
    lev_n = table.shape[0]
    shaped = table.reshape(lev_n, HEADS, WLEV, WLEV, WLAT, WLAT, 2 * WLON - 1)
    offsets = jnp.arange(WLON)
    relative = jnp.arange(2 * WLON - 1)
    picker = (
        relative[None, None, :] == offsets[:, None, None] - offsets[None, :, None] + WLON - 1
    ).astype(jnp.bfloat16)
    full_bias = jnp.einsum(
        "nhabcdr,xyr->nhacxbdy", shaped, picker, preferred_element_type=jnp.float32
    )
    tokens = WLEV * WLAT * WLON
    return full_bias.reshape(lev_n, HEADS, tokens, tokens)


def windows(grid):
    samples = grid.shape[0]
    width = grid.shape[-1]
    split = grid.reshape(samples, LEV // WLEV, WLEV, WLAT, LONW, WLON, width)
    split = split.transpose(0, 1, 4, 2, 3, 5, 6)
    return split.reshape(samples, LEV // WLEV, LONW, WLEV * WLAT * WLON, width)


def unwindows(windowed):
    samples = windowed.shape[0]
    width = windowed.shape[-1]
    split = windowed.reshape(samples, LEV // WLEV, LONW, WLEV, WLAT, WLON, width)
    split = split.transpose(0, 1, 3, 4, 2, 5, 6)
    return split.reshape(samples, LEV, WLAT, LONW * WLON, width)


def attend(windowed, w_qkv, w_proj, bias):
    width = windowed.shape[-1]
    head_size = width // HEADS
    scale = 1.0 / head_size**0.5
    leading = windowed.shape[:-1]
    as_float = windowed.astype(jnp.float32)
    mean_val = jnp.mean(as_float, axis=-1, keepdims=True)
    mean_removed = as_float - mean_val
    reciprocal_scale = lax.rsqrt(
        jnp.mean(mean_removed * mean_removed, axis=-1, keepdims=True) + 1e-05
    )
    standardized_input = mean_removed * reciprocal_scale
    normalized_input = standardized_input.astype(jnp.bfloat16)
    qkv_rows = jnp.dot(
        normalized_input.reshape(-1, width), w_qkv, preferred_element_type=jnp.float32
    ).astype(jnp.bfloat16)
    qkv_rows = qkv_rows.reshape(leading + (3, HEADS, head_size))
    query_matrix = qkv_rows[..., 0, :, :]
    key_matrix = qkv_rows[..., 1, :, :]
    value_matrix = qkv_rows[..., 2, :, :]
    scores = (
        jnp.einsum(
            "...qhd,...khd->...hqk", query_matrix, key_matrix, preferred_element_type=jnp.float32
        )
        * scale
        + bias
    )
    row_max = jnp.max(scores, axis=-1, keepdims=True)
    expo = jnp.exp(scores - row_max)
    attention_weights_matrix = expo / jnp.sum(expo, axis=-1, keepdims=True)
    weights_bfloat = attention_weights_matrix.astype(jnp.bfloat16)
    attended_values = jnp.einsum(
        "...hqk,...khd->...qhd", weights_bfloat, value_matrix, preferred_element_type=jnp.float32
    )
    attended_values = attended_values.astype(jnp.bfloat16).reshape(leading + (width,))
    projected = jnp.dot(
        attended_values.reshape(-1, width), w_proj, preferred_element_type=jnp.float32
    ).reshape(leading + (width,))
    block_output = (projected + as_float).astype(jnp.bfloat16)
    return (
        block_output,
        (
            standardized_input,
            reciprocal_scale,
            query_matrix,
            key_matrix,
            value_matrix,
            attention_weights_matrix,
            weights_bfloat,
            attended_values,
        ),
    )


def backprop(grad_out, stored_residuals, w_qkv, w_proj):
    (
        standardized_input,
        reciprocal_scale,
        query_matrix,
        key_matrix,
        value_matrix,
        attention_weights_matrix,
        weights_bfloat,
        attended_values,
    ) = stored_residuals
    width = grad_out.shape[-1]
    head_size = width // HEADS
    scale = 1.0 / head_size**0.5
    leading = grad_out.shape[:-1]
    flat_grad = grad_out.reshape(-1, width)
    grad_proj = lax.dot_general(
        attended_values.reshape(-1, width),
        flat_grad,
        (((0,), (0,)), ((), ())),
        preferred_element_type=jnp.float32,
    )
    grad_mixed = lax.dot_general(
        flat_grad, w_proj, (((1,), (1,)), ((), ())), preferred_element_type=jnp.float32
    ).astype(jnp.bfloat16)
    grad_mixed = grad_mixed.reshape(leading + (HEADS, head_size))
    grad_probs = jnp.einsum(
        "...qhd,...khd->...hqk", grad_mixed, value_matrix, preferred_element_type=jnp.float32
    )
    inner = jnp.sum(attention_weights_matrix * grad_probs, axis=-1, keepdims=True)
    grad_scores = (attention_weights_matrix * (grad_probs - inner)).astype(jnp.bfloat16)
    grad_values = jnp.einsum(
        "...hqk,...qhd->...khd", weights_bfloat, grad_mixed, preferred_element_type=jnp.float32
    ).astype(jnp.bfloat16)
    grad_query = (
        jnp.einsum(
            "...hqk,...khd->...qhd", grad_scores, key_matrix, preferred_element_type=jnp.float32
        )
        * scale
    ).astype(jnp.bfloat16)
    grad_keys = (
        jnp.einsum(
            "...hqk,...qhd->...khd", grad_scores, query_matrix, preferred_element_type=jnp.float32
        )
        * scale
    ).astype(jnp.bfloat16)
    grad_qkv = jnp.stack([grad_query, grad_keys, grad_values], axis=-3).reshape(-1, 3 * width)
    normalized_gradient = lax.dot_general(
        grad_qkv, w_qkv, (((1,), (1,)), ((), ())), preferred_element_type=jnp.float32
    )
    normalized_gradient = normalized_gradient.reshape(leading + (width,))
    average_gradient = jnp.mean(normalized_gradient, axis=-1, keepdims=True)
    average_product = jnp.mean(normalized_gradient * standardized_input, axis=-1, keepdims=True)
    input_gradient = reciprocal_scale * (
        normalized_gradient - average_gradient - standardized_input * average_product
    )
    return ((grad_out.astype(jnp.float32) + input_gradient).astype(jnp.bfloat16), grad_proj)


def halves(grid, dim, by, strip):
    length = grid.shape[dim]
    if by < 0:
        return (
            lax.slice_in_dim(grid, strip, length, axis=dim),
            lax.slice_in_dim(grid, 0, strip, axis=dim),
        )
    return (
        lax.slice_in_dim(grid, 0, length - strip, axis=dim),
        lax.slice_in_dim(grid, length - strip, length, axis=dim),
    )


def joined(kept, arrived, dim, by):
    if by < 0:
        return jnp.concatenate([kept, arrived], axis=dim)
    return jnp.concatenate([arrived, kept], axis=dim)


def move_strips(grid, by):
    row_strip = WLAT // 2
    col_strip = WLON // 2
    rows_keep, rows_send = halves(grid, 2, by, row_strip)
    arrived = shifted_2(rows_send, "lat", by)
    middle_grid = joined(rows_keep, arrived, 2, by)
    cols_keep, cols_send = halves(middle_grid, 3, by, col_strip)
    cols_got = shifted_2(cols_send, "lon", by)
    return joined(cols_keep, cols_got, 3, by)


def shift_in(grid):
    return move_strips(jnp.roll(grid, -(WLEV // 2), axis=1), -1)


def shift_back(grid):
    return jnp.roll(move_strips(grid, 1), WLEV // 2, axis=1)


def body(field, cotangent, qkv_plain, proj_plain, bias_plain, qkv_shift, proj_shift, bias_shift):
    full_plain, full_shift = (
        lax.all_gather(qkv_plain, "dp", axis=1, tiled=True),
        lax.all_gather(qkv_shift, "dp", axis=1, tiled=True),
    )
    lev_n = LEV // WLEV
    tokens = WLEV * WLAT * WLON
    bias_a = expand_bias(bias_plain[:, 0])
    bias_b = expand_bias(bias_shift[:, 0])
    lat_total = WLAT * lax.axis_size("lat")
    row_ids = lax.axis_index("lat") * WLAT + jnp.arange(WLAT)
    lat_label = (row_ids >= lat_total - WLAT // 2).astype(jnp.int32)
    lev_label = (jnp.arange(LEV) >= LEV - WLEV // 2).astype(jnp.int32)
    grid_label = (lev_label[:, None] * 2 + lat_label[None, :]).reshape(lev_n, WLEV, WLAT)
    grid_label = jnp.broadcast_to(grid_label[..., None], (lev_n, WLEV, WLAT, WLON)).reshape(
        lev_n, tokens
    )
    blocked = jnp.where(grid_label[:, :, None] == grid_label[:, None, :], 0.0, -1e30).astype(
        jnp.float32
    )
    bias_b = bias_b + blocked[:, None]
    first, saved_a = attend(windows(field), full_plain, proj_plain, bias_a[None, :, None])
    shifted = shift_in(unwindows(first))
    grad_moved = shift_in(cotangent)
    second, saved_b = attend(windows(shifted), full_shift, proj_shift, bias_b[None, :, None])
    out_field = shift_back(unwindows(second))
    grad_shifted, grad_proj_b = backprop(windows(grad_moved), saved_b, full_shift, proj_shift)
    grad_first = windows(shift_back(unwindows(grad_shifted)))
    grad_field, grad_proj_a = backprop(grad_first, saved_a, full_plain, proj_plain)
    grad_proj_a, grad_proj_b = lax.psum((grad_proj_a, grad_proj_b), ("lat", "lon", "dp"))
    return (
        out_field,
        unwindows(grad_field),
        grad_proj_a.astype(jnp.bfloat16),
        grad_proj_b.astype(jnp.bfloat16),
    )


def solution(mesh):
    placed = (
        P("dp", None, "lat", "lon", None),
        P("dp", None, "lat", "lon", None),
        P(None, "dp"),
        P(),
        P(None, "lat", None, None),
        P(None, "dp"),
        P(),
        P(None, "lat", None, None),
    )
    return jax.shard_map(
        body,
        mesh=mesh,
        in_specs=placed,
        out_specs=(P("dp", None, "lat", "lon", None), P("dp", None, "lat", "lon", None), P(), P()),
        check_vma=False,
    )
```

profile of v0, /device:TPU:1, one launch (start us, length us, event | category | flops | bytes accessed | tf_op | source)
XLA Modules:
  0.0 349.9 jit_solution(2405594267803422785)
XLA Ops:
  2.7 6.9 %collective-permute-start.4 = (bf16[1,2,6,6,384]{4,1,3,2,0:T(2,128)(2,1)}, bf16[1,2,6,6,384]{4,1,3,2,0:T(2,128)(2,1)}, u32[]{:S(2)}, u32[]{:S(2)}) collective-permute-start(bf16[1,2,6,6,384]{4,1,3,2,0:T(2,128)(2,1)} %get-tuple-element.31), channel_id=1, source_target_pairs={{0,448},{64,0},{128,64},{192,128},{256,192},{320,256},{384,320},{4... | collective-permute-start | bytes 165896 | tf_op jit(solution)/shard_map/ppermute | solution.py:16
  13.0 1.9 multiply_reduce_fusion.5
  15.0 14.0 %all_gather.6 = bf16[384,1152]{0,1:T(8,128)(2,1)S(1)} all-gather(bf16[384,576]{0,1:T(8,128)(2,1)S(1)} %copy-done.19), channel_id=1, replica_groups=mesh['lat'=8,'lon'=32,'dp'=2] {'dp'}, dimensions={1}, use_global_device_ids=true | all-gather | bytes 1327104 | tf_op jit(solution)/shard_map/all_gather | solution.py:203
  30.6 3.4 reshape.580
  34.0 11.8 %convolution_bitcast_fusion.1 = f32[1,12,2,12,6,2,12,6]{6,7,3,5,2,1,4,0:T(8,128)} fusion(bf16[12,2,2,12,12,11,1]{5,4,3,2,1,0,6:T(8,128)(2,1)S(1)} %reshape.580, s32[6,6]{1,0:T(8,128)S(1)} %subtract_add_fusion), kind=kOutput, calls=%fused_computation.3 | convolution fusion | flops 5474700 | bytes 1147536 | tf_op jit(solution)/shard_map/nhabcdr,xyr->nhacxbdy/dot_general | solution.py:27
  45.8 18.9 %copy.110 = f32[1,12,2,12,6,2,12,6]{1,7,6,5,4,3,2,0:T(8,128)} copy(f32[1,12,2,12,6,2,12,6]{6,7,3,5,2,1,4,0:T(8,128)} %convolution_bitcast_fusion.1) | data formatting | bytes 1990656 | tf_op jit(solution)/shard_map/nhabcdr,xyr->nhacxbdy/transpose | solution.py:27
  64.7 13.1 %broadcast_in_dim_reshape.2 = f32[12,144,144]{0,2,1:T(8,128)} reshape(f32[1,12,2,12,6,2,12,6]{1,7,6,5,4,3,2,0:T(8,128)} %copy.110) | data formatting | bytes 1990656 | tf_op jit(solution)/shard_map/broadcast_in_dim;reshape | solution.py:222
  77.8 12.2 %copy.111 = f32[12,144,144]{1,2,0:T(8,128)} copy(f32[12,144,144]{0,2,1:T(8,128)} %broadcast_in_dim_reshape.2) | data formatting | bytes 1990656 | tf_op jit(solution)/shard_map/broadcast_in_dim;reshape | solution.py:222
  90.0 1.9 multiply_add_fusion
  91.9 1.9 fusion.50
  93.8 2.2 convolution_convert_fusion.5
  99.7 3.4 reshape.581
  103.2 11.8 %convolution_bitcast_fusion = f32[1,12,2,12,6,2,12,6]{6,7,3,5,2,1,4,0:T(8,128)} fusion(bf16[12,2,2,12,12,11,1]{5,4,3,2,1,0,6:T(8,128)(2,1)S(1)} %reshape.581, s32[6,6]{1,0:T(8,128)S(1)} %subtract_add_fusion), kind=kOutput, calls=%fused_computation.2 | convolution fusion | flops 5474700 | bytes 1147536 | tf_op jit(solution)/shard_map/nhabcdr,xyr->nhacxbdy/dot_general | solution.py:27
  115.0 14.0 %all_gather.7 = bf16[384,1152]{0,1:T(8,128)(2,1)S(1)} all-gather(bf16[384,576]{0,1:T(8,128)(2,1)S(1)} %copy-done.20), channel_id=1, replica_groups=mesh['lat'=8,'lon'=32,'dp'=2] {'dp'}, dimensions={1}, use_global_device_ids=true | all-gather | bytes 1327104 | tf_op jit(solution)/shard_map/all_gather | solution.py:204
  128.9 18.9 %copy.116 = f32[1,12,2,12,6,2,12,6]{1,7,6,5,4,3,2,0:T(8,128)} copy(f32[1,12,2,12,6,2,12,6]{6,7,3,5,2,1,4,0:T(8,128)} %convolution_bitcast_fusion) | data formatting | bytes 1990656 | tf_op jit(solution)/shard_map/nhabcdr,xyr->nhacxbdy/transpose | solution.py:27
  147.8 13.1 %reshape.570 = f32[12,144,144]{0,2,1:T(8,128)} reshape(f32[1,12,2,12,6,2,12,6]{1,7,6,5,4,3,2,0:T(8,128)} %copy.116) | data formatting | bytes 1990656 | tf_op jit(solution)/shard_map/reshape | solution.py:31
  161.0 12.2 %copy.117 = f32[12,144,144]{1,2,0:T(8,128)} copy(f32[12,144,144]{0,2,1:T(8,128)} %reshape.570) | data formatting | bytes 1990656 | tf_op jit(solution)/shard_map/reshape | solution.py:31
  174.2 4.4 %collective-permute-start.1 = (bf16[1,2,12,3,384]{4,3,2,1,0:T(4,128)(2,1)S(1)}, bf16[1,2,12,3,384]{4,3,2,1,0:T(4,128)(2,1)S(1)}, u32[]{:S(2)}, u32[]{:S(2)}) collective-permute-start(bf16[1,2,12,3,384]{4,3,2,1,0:T(4,128)(2,1)S(1)} %get-tuple-element.41), channel_id=1, source_target_pairs={{0,62},{2,0},{4,2},{6,4},{8,6},{10,8},{12,10},{14,12},{16,14},{18,... | collective-permute-start | bytes 165896 | tf_op jit(solution)/shard_map/ppermute | solution.py:16
  179.5 2.9 collective-permute-start.5
  184.9 1.9 multiply_reduce_fusion.4
  189.3 2.2 add_add_fusion
  193.2 2.5 convolution_convert_fusion.4
  198.2 3.2 fusion.6
  201.4 2.1 multiply_reduce_fusion.1
  208.8 5.7 %collective-permute-start.6 = (bf16[1,2,6,6,384]{4,3,2,1,0:T(8,128)(2,1)S(1)}, bf16[1,2,6,6,384]{4,3,2,1,0:T(8,128)(2,1)S(1)}, u32[]{:S(2)}, u32[]{:S(2)}) collective-permute-start(bf16[1,2,6,6,384]{4,3,2,1,0:T(8,128)(2,1)S(1)} %get-tuple-element.34), channel_id=1, source_target_pairs={{0,64},{64,128},{128,192},{192,256},{256,320},{320,384},{384,448},... | collective-permute-start | bytes 165896 | tf_op jit(solution)/shard_map/ppermute | solution.py:16
  216.0 1.9 collective-permute-start.7
  218.6 1.9 collective-permute-start.3
  220.6 2.6 collective-permute-done.7
  225.6 1.9 convolution_convert_fusion.6
  227.5 2.0 fusion.52
  234.0 2.6 fusion.7
  240.2 109.7 %all-reduce.2 = (bf16[384,384]{1,0:T(8,128)(2,1)}, bf16[384,384]{1,0:T(8,128)(2,1)}) all-reduce(f32[384,384]{1,0:T(8,128)S(1)} %copy-done.13, f32[384,384]{1,0:T(8,128)S(1)} %copy-done.12), channel_id=1, replica_groups=mesh['lat'=8,'lon'=32,'dp'=2] {'lat','lon','dp'}, use_global_device_ids=true, to_apply=%region_14.15 | all-reduce | flops 294912 | bytes 1769472 | tf_op jit(solution)/shard_map/psum | solution.py:230
  (148 shorter events, 39.5 us)
Async XLA Ops:
  0.6 195.1 %copy-start = (bf16[384,384]{1,0:T(8,128)(2,1)S(1)}, bf16[384,384]{1,0:T(8,128)(2,1)}, u32[]{:S(2)}) copy-start(bf16[384,384]{1,0:T(8,128)(2,1)} %param.14) | copy-start | bytes 884740
  0.6 14.3 %copy-start.19 = (bf16[384,576]{0,1:T(8,128)(2,1)S(1)}, bf16[384,576]{0,1:T(8,128)(2,1)}, u32[]{:S(2)}) copy-start(bf16[384,576]{0,1:T(8,128)(2,1)} %param.10) | copy-start | bytes 1327108
  2.7 175.8 %collective-permute-start.4 = (bf16[1,2,6,6,384]{4,1,3,2,0:T(2,128)(2,1)}, bf16[1,2,6,6,384]{4,1,3,2,0:T(2,128)(2,1)}, u32[]{:S(2)}, u32[]{:S(2)}) collective-permute-start(bf16[1,2,6,6,384]{4,1,3,2,0:T(2,128)(2,1)} %get-tuple-element.31), channel_id=1, source_target_pairs={{0,448},{64,0},{128,64},{192,128},{256,192},{320,256},{384,320},{4... | collective-permute-start | bytes 165896 | tf_op jit(solution)/shard_map/ppermute | solution.py:16
  13.0 16.5 %copy-start.28 = (f32[144]{0:T(256)}, f32[144]{0:T(256)S(1)}, u32[]{:S(2)}) copy-start(f32[144]{0:T(256)S(1)} %div.47) | copy-start | bytes 1732
  14.9 14.5 %copy-start.30 = (f32[144]{0:T(256)}, f32[144]{0:T(256)S(1)}, u32[]{:S(2)}) copy-start(f32[144]{0:T(256)S(1)} %add_rsqrt_fusion.1) | copy-start | bytes 1732
  15.0 14.5 %copy-start.5 = (f32[144,384]{1,0:T(8,128)}, f32[144,384]{1,0:T(8,128)S(1)}, u32[]{:S(2)}) copy-start(f32[144,384]{1,0:T(8,128)S(1)} %reshape.575) | copy-start | bytes 663556
  77.8 12.2 %copy-start.8 = (bf16[144,1152]{0,1:T(8,128)(2,1)S(1)}, bf16[144,1152]{0,1:T(8,128)(2,1)}, u32[]{:S(2)}) copy-start(bf16[144,1152]{0,1:T(8,128)(2,1)} %copy.109) | copy-start | bytes 995332
  93.7 2.2 copy-start.26
  93.8 2.2 copy-start.6
  93.8 2.2 copy-start.15
  98.0 75.2 %collective-permute-start = (bf16[1,2,6,6,384]{4,3,2,1,0:T(8,128)(2,1)}, bf16[1,2,6,6,384]{4,3,2,1,0:T(8,128)(2,1)}, u32[]{:S(2)}, u32[]{:S(2)}) collective-permute-start(bf16[1,2,6,6,384]{4,3,2,1,0:T(8,128)(2,1)} %get-tuple-element.43), channel_id=1, source_target_pairs={{0,448},{64,0},{128,64},{192,128},{256,192},{320,256},{384,320},{4... | collective-permute-start | bytes 165896 | tf_op jit(solution)/shard_map/ppermute | solution.py:16
  103.2 11.8 %copy-start.20 = (bf16[384,576]{0,1:T(8,128)(2,1)S(1)}, bf16[384,576]{0,1:T(8,128)(2,1)}, u32[]{:S(2)}) copy-start(bf16[384,576]{0,1:T(8,128)(2,1)} %param.13) | copy-start | bytes 1327108
  161.0 12.2 %copy-start.23 = (bf16[1,2,6,6,384]{4,3,2,1,0:T(8,128)(2,1)S(1)}, bf16[1,2,6,6,384]{4,3,2,1,0:T(8,128)(2,1)}, u32[]{:S(2)}) copy-start(bf16[1,2,6,6,384]{4,3,2,1,0:T(8,128)(2,1)} %get-tuple-element.42) | copy-start | bytes 165892
  161.0 17.6 %copy-start.24 = (bf16[1,2,6,6,384]{4,1,3,2,0:T(2,128)(2,1)S(1)}, bf16[1,2,6,6,384]{4,1,3,2,0:T(2,128)(2,1)}, u32[]{:S(2)}) copy-start(bf16[1,2,6,6,384]{4,1,3,2,0:T(2,128)(2,1)} %get-tuple-element.30) | copy-start | bytes 165892
  174.2 8.2 %collective-permute-start.1 = (bf16[1,2,12,3,384]{4,3,2,1,0:T(4,128)(2,1)S(1)}, bf16[1,2,12,3,384]{4,3,2,1,0:T(4,128)(2,1)S(1)}, u32[]{:S(2)}, u32[]{:S(2)}) collective-permute-start(bf16[1,2,12,3,384]{4,3,2,1,0:T(4,128)(2,1)S(1)} %get-tuple-element.41), channel_id=1, source_target_pairs={{0,62},{2,0},{4,2},{6,4},{8,6},{10,8},{12,10},{14,12},{16,14},{18,... | collective-permute-start | bytes 165896 | tf_op jit(solution)/shard_map/ppermute | solution.py:16
  179.5 4.9 %collective-permute-start.5 = (bf16[1,2,12,3,384]{4,1,3,2,0:T(2,128)(2,1)S(1)}, bf16[1,2,12,3,384]{4,1,3,2,0:T(2,128)(2,1)S(1)}, u32[]{:S(2)}, u32[]{:S(2)}) collective-permute-start(bf16[1,2,12,3,384]{4,1,3,2,0:T(2,128)(2,1)S(1)} %get-tuple-element.47), channel_id=1, source_target_pairs={{0,62},{2,0},{4,2},{6,4},{8,6},{10,8},{12,10},{14,12},{16,14},{18,... | collective-permute-start | bytes 165896 | tf_op jit(solution)/shard_map/ppermute | solution.py:16
  184.4 4.9 %copy-start.18 = (f32[144,144]{0,1:T(8,128)S(1)}, f32[144,144]{0,1:T(8,128)}, u32[]{:S(2)}) copy-start(f32[144,144]{0,1:T(8,128)} %compare_select_fusion) | copy-start | bytes 248836
  189.3 12.1 %copy-start.10 = (bf16[144,1152]{0,1:T(8,128)(2,1)}, bf16[144,1152]{0,1:T(8,128)(2,1)S(1)}, u32[]{:S(2)}) copy-start(bf16[144,1152]{0,1:T(8,128)(2,1)S(1)} %copy.115) | copy-start | bytes 995332
  201.4 2.1 copy-start.2
  208.8 7.1 %collective-permute-start.6 = (bf16[1,2,6,6,384]{4,3,2,1,0:T(8,128)(2,1)S(1)}, bf16[1,2,6,6,384]{4,3,2,1,0:T(8,128)(2,1)S(1)}, u32[]{:S(2)}, u32[]{:S(2)}) collective-permute-start(bf16[1,2,6,6,384]{4,3,2,1,0:T(8,128)(2,1)S(1)} %get-tuple-element.34), channel_id=1, source_target_pairs={{0,64},{64,128},{128,192},{192,256},{256,320},{320,384},{384,448},... | collective-permute-start | bytes 165896 | tf_op jit(solution)/shard_map/ppermute | solution.py:16
  214.5 3.4 copy-start.16
  214.5 16.7 %copy-start.1 = (f32[12,144,144]{1,2,0:T(8,128)S(1)}, f32[12,144,144]{1,2,0:T(8,128)}, u32[]{:S(2)}) copy-start(f32[12,144,144]{1,2,0:T(8,128)} %get-tuple-element.51) | copy-start | bytes 2985988
  214.5 16.7 %copy-start.9 = (bf16[144,1152]{0,1:T(8,128)(2,1)S(1)}, bf16[144,1152]{0,1:T(8,128)(2,1)}, u32[]{:S(2)}) copy-start(bf16[144,1152]{0,1:T(8,128)(2,1)} %copy.109) | copy-start | bytes 995332
  214.6 16.7 %copy-start.27 = (f32[12,144]{1,0:T(8,128)S(1)}, f32[12,144]{1,0:T(8,128)}, u32[]{:S(2)}) copy-start(f32[12,144]{1,0:T(8,128)} %copy-done.26) | copy-start | bytes 20740
  214.6 3.4 collective-permute-start.2
  216.0 7.2 %collective-permute-start.7 = (bf16[1,2,12,3,384]{4,3,2,1,0:T(4,128)(2,1)S(1)}, bf16[1,2,12,3,384]{4,3,2,1,0:T(4,128)(2,1)S(1)}, u32[]{:S(2)}, u32[]{:S(2)}) collective-permute-start(bf16[1,2,12,3,384]{4,3,2,1,0:T(4,128)(2,1)S(1)} %fusion.30), channel_id=1, source_target_pairs={{0,2},{2,4},{4,6},{6,8},{8,10},{10,12},{12,14},{14,16},{16,18},{18... | collective-permute-start | bytes 165896 | tf_op jit(solution)/shard_map/ppermute | solution.py:16
  217.9 2.6 copy-start.21
  218.6 18.0 %collective-permute-start.3 = (bf16[1,2,12,3,384]{4,3,2,1,0:T(4,128)(2,1)}, bf16[1,2,12,3,384]{4,3,2,1,0:T(4,128)(2,1)}, u32[]{:S(2)}, u32[]{:S(2)}) collective-permute-start(bf16[1,2,12,3,384]{4,3,2,1,0:T(4,128)(2,1)} %fusion.31), channel_id=1, source_target_pairs={{0,2},{2,4},{4,6},{6,8},{8,10},{10,12},{12,14},{14,16},{16,18},{18... | collective-permute-start | bytes 165896 | tf_op jit(solution)/shard_map/ppermute | solution.py:16
  234.0 2.6 copy-start.17
  234.0 2.6 copy-start.22
  236.6 2.1 copy-start.7
  236.6 2.1 copy-start.29
  (8 other events, 12.4 us)
where the time goes:
time: 352 us; the launch traced here: 350 us
  blocking collectives  138 us (39%)
  local copies, waits for them, and re-layouts  109 us (31%)
  matrix products  53.8 us (15%)
  starting transfers between devices  24.5 us (7%)
  other arithmetic  18.3 us (5%)
  waiting for transfers between devices  5.62 us (2%)
    psum x1, blocking collectives, body(): lax.psum((grad_proj_a, grad_proj_b), ('lat', 'lon', 'dp'))  110 us
    transpose x2, local copies, waits for them, and re-layouts, expand_bias(): jnp.einsum('nhabcdr,xyr->nhacxbdy', shaped, picker, preferred_element_typ...  37.8 us
    reshape x2, local copies, waits for them, and re-layouts, expand_bias(): return full_bias.reshape(lev_n, HEADS, tokens, tokens)  25.3 us
    another operation x2, local copies, waits for them, and re-layouts, body(): bias_a[None, :, None]  25.3 us
    ppermute x8, starting transfers between devices, shifted_2(): lax.ppermute(x, axis, [(i, (i + by) % length) for i in range(length)])  24.5 us
    dot_general x2, matrix products, expand_bias(): jnp.einsum('nhabcdr,xyr->nhacxbdy', shaped, picker, preferred_element_typ...  23.5 us
    all_gather x1, blocking collectives, body(): lax.all_gather(qkv_plain, 'dp', axis=1, tiled=True)  14 us
    all_gather x1, blocking collectives, body(): lax.all_gather(qkv_shift, 'dp', axis=1, tiled=True)  14 us
  transfers between devices with their start and end apart: 8, of which 3 were waited for; matrix products, arithmetic and copies ran while one was open for 43% of the time, Pallas kernels for 0%

commit v1 on v0

v1 whole, which is shorter than its diff:
```python
import functools

import jax
import jax.numpy as jnp
import numpy as np
from jax import lax
from jax.experimental import pallas as pl
from jax.experimental.pallas import tpu as pltpu
from jax.sharding import PartitionSpec as P

HEADS = 12
HEAD = 32
C = 384
LEV = 2
WLAT = 12
WLON = 6
TOKENS = LEV * WLAT * WLON
QUAD = 48
GROUPS = 3
PER = HEADS // GROUPS
REL = 2 * WLON - 1
CHUNK = WLAT * REL
MESH = pl.DeviceIdType.MESH
F32 = jnp.float32
BF16 = jnp.bfloat16


def nn(a, b):
    return lax.dot_general(a, b, (((1,), (0,)), ((), ())), preferred_element_type=F32)


def nt(a, b):
    return lax.dot_general(a, b, (((1,), (1,)), ((), ())), preferred_element_type=F32)


def token(h, w, z):
    return (h * WLON + w) * LEV + z


def constants():
    gather = np.zeros((TOKENS, 4 * QUAD), np.float32)
    pick = np.zeros((TOKENS, 256), np.float32)
    for h in range(WLAT):
        for w in range(WLON):
            for z in range(LEV):
                slot = (h // 6) * 2 + w // 3
                inner = ((h % 6) * 3 + w % 3) * 2 + (1 - z)
                gather[token(h, w, z), slot * QUAD + inner] = 1
                pick[token(h, w, z), z * 127 + h * REL + WLON - 1 - w] = 1
    scatter = np.zeros((4 * QUAD, TOKENS), np.float32)
    for h in range(WLAT):
        for w in range(WLON):
            for z in range(LEV):
                slot = (h // 6) * 2 + w // 3
                scatter[slot * QUAD + ((h % 6) * 3 + w % 3) * 2 + z, token(h, w, z)] = 1
    return gather, scatter, pick


def kernel(
    sizes,
    field,
    cot,
    wp_half,
    ws_half,
    proj_p,
    proj_s,
    tab_p,
    tab_s,
    gather,
    scatter,
    pick,
    out_field,
    out_grad,
    gp_p,
    gp_s,
    wp,
    ws,
    xf,
    quads,
    xhat_p,
    rstd_p,
    xhat_s,
    rstd_s,
    s2f,
    dy2f,
    qkv_p,
    kvt_p,
    qkv_s,
    kvt_s,
    probs_p,
    ot_p,
    ot_s,
    dqkv,
    dqt,
    bias_p,
    bias_s,
    tabf,
    spread,
    send,
    recv,
    halo_ss,
    halo_rs,
    own_sem,
    w_ss,
    w_rs,
    f_ss,
    f_rs,
):
    n_lat, n_lon, n_dp = sizes
    lat, lon, dp = lax.axis_index("lat"), lax.axis_index("lon"), lax.axis_index("dp")
    core = lax.rem(lat, 2)
    sibling = (lat + 1 - 2 * core, lon, dp)
    across = (lat, lax.rem(lon + n_lon // 2, n_lon), 1 - dp)

    def near(dlat, dlon):
        return (
            lax.rem(lat + dlat + n_lat, n_lat),
            lax.rem(lon + dlon + n_lon, n_lon),
            dp,
        )

    greet = [sibling, across]
    greet += [near(a, b) for a, b in ((1, 0), (0, 1), (1, 1), (-1, 0), (0, -1), (-1, -1))]
    barrier = pltpu.get_barrier_semaphore()
    for device in greet:
        pl.semaphore_signal(barrier, inc=1, device_id=device, device_id_type=MESH)
    own = [
        pltpu.make_async_copy(wp_half, wp.at[dp], own_sem.at[0]),
        pltpu.make_async_copy(ws_half, ws.at[dp], own_sem.at[1]),
    ]
    for copy in own:
        copy.start()
    pl.semaphore_wait(barrier, len(greet))

    rows = pl.ds(pl.multiple_of(core * 288, 32), 288)

    def weights_across(half, full, i):
        return pltpu.make_async_remote_copy(
            half.at[rows],
            full.at[dp, rows],
            w_ss.at[i],
            w_rs.at[i],
            device_id=across,
            device_id_type=MESH,
        )

    def weights_beside(full, i):
        part = full.at[1 - dp, rows]
        return pltpu.make_async_remote_copy(
            part, part, f_ss.at[i], f_rs.at[i], device_id=sibling, device_id_type=MESH
        )

    first = [weights_across(wp_half, wp, 0), weights_across(ws_half, ws, 1)]
    for copy in first:
        copy.start()
    beside = [weights_beside(wp, 0), weights_beside(ws, 1)]

    def halo(i, by):
        kept = 3 if by < 0 else 0
        copies = []
        for slot in range(4):
            if slot == kept:
                recv[i, 3 - slot] = send[i, slot]
                continue
            a, b = divmod(slot, 2)
            moves = 0 if by < 0 else 1
            copies.append(
                pltpu.make_async_remote_copy(
                    send.at[i, slot],
                    recv.at[i, 3 - slot],
                    halo_ss.at[i, slot],
                    halo_rs.at[i, 3 - slot],
                    device_id=near(by if a == moves else 0, by if b == moves else 0),
                    device_id_type=MESH,
                )
            )
        for copy in copies:
            copy.start()
        return copies

    def arrived(i, copies):
        for copy in copies:
            copy.wait_recv()
        return nn(gather[...], recv[i].reshape(4 * QUAD, C))

    def to_quads(i, x):
        send[i] = nn(scatter[...], x).astype(BF16).reshape(4, QUAD, C)

    quads[...] = jnp.zeros_like(quads)
    for h in range(WLAT):
        for w in range(WLON):
            at = ((h // 6) * 2 + w // 3) * QUAD + ((h % 6) * 3 + w % 3) * 2
            quads[at : at + 2, :] = cot[h * WLON + w].astype(F32)
    send[0] = quads[...].astype(BF16).reshape(4, QUAD, C)
    halo_cot = halo(0, -1)

    for i in range(WLAT * WLON):
        xf[2 * i : 2 * i + 2, :] = field[i].astype(F32)

    def norm(x, xhat, rstd):
        mean = jnp.mean(x, axis=-1, keepdims=True)
        centred = x - mean
        r = lax.rsqrt(jnp.mean(centred * centred, axis=-1, keepdims=True) + 1e-5)
        y = centred * r
        xhat[...] = y
        rstd[...] = r
        return y.astype(BF16)

    lane256 = lax.broadcasted_iota(jnp.int32, (16, 256), 1)

    def expand(tab, bias, hide):
        tabf[...] = jnp.zeros_like(tabf)
        tabf[0:HEADS, 0 : 4 * WLAT * CHUNK] = tab[...].astype(F32)

        def row(h, carry):
            for za in range(LEV):
                parts = []
                for zb in range(LEV):
                    c = (za * 2 + zb) * WLAT + h
                    tile = c + c // 32
                    off = 4 * lax.rem(c, 32)
                    window = tabf[:, pl.ds(pl.multiple_of(tile * 128, 128), 256)]
                    parts.append(pltpu.roll(window, lax.rem(256 + 127 * zb - off, 256), 1))
                for w in range(WLON):
                    low, high = parts
                    if w:
                        low = pltpu.roll(low, 256 - w, 1)
                        high = pltpu.roll(high, 256 - w, 1)
                    at = pl.multiple_of((h * WLON + w) * 32 + za * 16, 16)
                    both = jnp.where(lane256 < 127, low, high)
                    spread[0, pl.ds(at, 16), :] = both[:, :128]
                    spread[1, pl.ds(at, 16), :] = both[:, 128:]
            return carry

        lax.fori_loop(0, WLAT, row, 0)
        for head in range(HEADS):
            lanes = [spread[half, pl.ds(head, TOKENS, stride=16), :] for half in range(2)]
            table = jnp.concatenate(lanes, axis=1).astype(BF16)
            full = nt(pick[...], table)
            bias[head] = full if hide is None else full + hide

    lane = lax.broadcasted_iota(jnp.int32, (TOKENS, 128), 1) // HEAD

    def by_head(x):
        zero = jnp.zeros_like(x)
        return jnp.concatenate([jnp.where(lane == j, x, zero) for j in range(PER)], axis=0)

    def own_lanes(x):
        total = jnp.where(lane == 0, x[0:TOKENS], 0.0)
        for j in range(1, PER):
            total += jnp.where(lane == j, x[j * TOKENS : (j + 1) * TOKENS], 0.0)
        return total

    scale = 1.0 / HEAD**0.5

    def project(n, full, qkv, kvt):
        w = full[...].reshape(3 * C, C)
        qkv[...] = nt(n, w).astype(BF16)
        kvt[...] = nt(w[C:], n).astype(BF16)

    def softmax(g, qkv, bias):
        q = qkv[:, g * 128 : (g + 1) * 128]
        k = qkv[:, C + g * 128 : C + (g + 1) * 128]
        s = nt(by_head(k), q).reshape(PER, TOKENS, TOKENS) * scale
        s = s + bias[g * PER : (g + 1) * PER]
        e = jnp.exp(s - jnp.max(s, axis=1, keepdims=True))
        return e / jnp.sum(e, axis=1, keepdims=True)

    def values(g, p, kvt, ot):
        for j in range(PER):
            at = g * 128 + j * HEAD
            vt = kvt[C + at : C + at + HEAD, :]
            ot[at : at + HEAD, :] = nn(vt, p[j]).astype(BF16)

    def grads(g, p, pb, do, qkv, kvt):
        cols = slice(g * 128, (g + 1) * 128)
        q = qkv[:, cols]
        v = qkv[:, 2 * C + g * 128 : 2 * C + (g + 1) * 128]
        dog = do[:, cols]
        dp_ = nt(by_head(v), dog).reshape(PER, TOKENS, TOKENS)
        inner = jnp.sum(p * dp_, axis=1, keepdims=True)
        ds = (p * (dp_ - inner)).astype(BF16)
        dv = own_lanes(nn(pb.reshape(PER * TOKENS, TOKENS), dog))
        dk = own_lanes(nn(ds.reshape(PER * TOKENS, TOKENS), q)) * scale
        dqkv[:, 2 * C + g * 128 : 2 * C + (g + 1) * 128] = dv.astype(BF16)
        dqkv[:, C + g * 128 : C + (g + 1) * 128] = dk.astype(BF16)
        for j in range(PER):
            at = g * 128 + j * HEAD
            dqt[at : at + HEAD, :] = nn(kvt[at : at + HEAD, :], ds[j]) * scale

    def input_grad(dy, full, xhat, rstd):
        dqkv[:, 0:C] = dqt[...].T.astype(BF16)
        dn = nn(dqkv[...], full[...].reshape(3 * C, C))
        xh = xhat[...]
        mean = jnp.mean(dn, axis=-1, keepdims=True)
        product = jnp.mean(dn * xh, axis=-1, keepdims=True)
        return (dy + rstd[...] * (dn - mean - xh * product)).astype(BF16)

    def output(x, ot, proj):
        o = ot[...].astype(F32).T.astype(BF16)
        return (x + nn(o, proj[...])).astype(BF16)

    n1 = norm(xf[...], xhat_p, rstd_p)
    expand(tab_p, bias_p, None)
    own[0].wait()
    first[0].wait_recv()
    beside[0].start()
    beside[0].wait_recv()
    project(n1, wp, qkv_p, kvt_p)
    for g in range(GROUPS):
        p = softmax(g, qkv_p, bias_p)
        probs_p[g * PER : (g + 1) * PER] = p
        values(g, p.astype(BF16), kvt_p, ot_p)
    h1 = output(xf[...], ot_p, proj_p)
    to_quads(1, h1)
    halo_h1 = halo(1, -1)

    key = lax.broadcasted_iota(jnp.int32, (TOKENS, TOKENS), 0)
    query = lax.broadcasted_iota(jnp.int32, (TOKENS, TOKENS), 1)
    edge = jnp.where(lat == n_lat - 1, TOKENS // 2, TOKENS)
    same = ((key & 1) == (query & 1)) & ((key >= edge) == (query >= edge))
    expand(tab_s, bias_s, jnp.where(same, 0.0, -1e30))
    own[1].wait()
    first[1].wait_recv()
    beside[1].start()
    dy2 = arrived(0, halo_cot)
    dy2f[...] = dy2
    do2 = nt(dy2.astype(BF16), proj_s[...]).astype(BF16)
    beside[1].wait_recv()

    s2 = arrived(1, halo_h1)
    s2f[...] = s2
    n2 = norm(s2, xhat_s, rstd_s)
    project(n2, ws, qkv_s, kvt_s)
    for g in range(GROUPS):
        p = softmax(g, qkv_s, bias_s)
        pb = p.astype(BF16)
        values(g, pb, kvt_s, ot_s)
        grads(g, p, pb, do2, qkv_s, kvt_s)
    ds2 = input_grad(dy2f[...], ws, xhat_s, rstd_s)
    to_quads(2, ds2)
    halo_g1 = halo(2, 1)

    y2 = output(s2f[...], ot_s, proj_s)
    to_quads(3, y2)
    halo_out = halo(3, 1)
    gp_s[...] = nn(ot_s[...], dy2f[...].astype(BF16))

    g1 = arrived(2, halo_g1)
    g1b = g1.astype(BF16)
    gp_p[...] = nn(ot_p[...], g1b)
    do1 = nt(g1b, proj_p[...]).astype(BF16)
    for g in range(GROUPS):
        p = probs_p[g * PER : (g + 1) * PER]
        grads(g, p, p.astype(BF16), do1, qkv_p, kvt_p)
    xf[...] = input_grad(g1, wp, xhat_p, rstd_p).astype(F32)
    for i in range(WLAT * WLON):
        out_grad[i] = xf[2 * i : 2 * i + 2, :].astype(BF16)
    s2f[...] = arrived(3, halo_out)
    for i in range(WLAT * WLON):
        out_field[i] = s2f[2 * i : 2 * i + 2, :].astype(BF16)

    for copies in (halo_cot, halo_h1, halo_g1, halo_out, first, beside):
        for copy in copies:
            copy.wait_send()


def body(sizes, field, cotangent, qkv_plain, proj_plain, bias_plain, qkv_shift, proj_shift, bias_shift):
    def rows(x):
        return x.transpose(0, 2, 3, 1, 4).reshape(WLAT * WLON, LEV, C)

    gather, scatter, pick = constants()
    operands = (
        rows(field),
        rows(cotangent),
        qkv_plain.T,
        qkv_shift.T,
        proj_plain,
        proj_shift,
        bias_plain.reshape(HEADS, -1),
        bias_shift.reshape(HEADS, -1),
        jnp.asarray(gather, BF16),
        jnp.asarray(scatter, BF16),
        jnp.asarray(pick, BF16),
    )
    vmem = pl.BlockSpec(memory_space=pltpu.VMEM)
    hbm = pl.BlockSpec(memory_space=pl.ANY)
    grid_shape = jax.ShapeDtypeStruct((WLAT * WLON, LEV, C), BF16)
    square = jax.ShapeDtypeStruct((C, C), F32)
    tokens_f32 = pltpu.VMEM((TOKENS, C), F32)
    row_stat = pltpu.VMEM((TOKENS, 1), F32)
    full_bias = pltpu.VMEM((HEADS, TOKENS, TOKENS), F32)
    out_field, out_grad, gp_p, gp_s = pl.pallas_call(
        functools.partial(kernel, sizes),
        out_shape=(grid_shape, grid_shape, square, square),
        in_specs=[vmem, vmem, hbm, hbm] + [vmem] * 7,
        out_specs=(vmem, vmem, vmem, vmem),
        scratch_shapes=[
            pltpu.VMEM((2, 3 * C // 2, C), BF16),
            pltpu.VMEM((2, 3 * C // 2, C), BF16),
            tokens_f32,
            pltpu.VMEM((4 * QUAD, C), F32),
            tokens_f32,
            row_stat,
            tokens_f32,
            row_stat,
            tokens_f32,
            tokens_f32,
            pltpu.VMEM((TOKENS, 3 * C), BF16),
            pltpu.VMEM((2 * C, TOKENS), BF16),
            pltpu.VMEM((TOKENS, 3 * C), BF16),
            pltpu.VMEM((2 * C, TOKENS), BF16),
            full_bias,
            pltpu.VMEM((C, TOKENS), BF16),
            pltpu.VMEM((C, TOKENS), BF16),
            pltpu.VMEM((TOKENS, 3 * C), BF16),
            pltpu.VMEM((C, TOKENS), F32),
            full_bias,
            full_bias,
            pltpu.VMEM((16, 6400), F32),
            pltpu.VMEM((2, TOKENS * 16, 128), F32),
            pltpu.VMEM((4, 4, QUAD, C), BF16),
            pltpu.VMEM((4, 4, QUAD, C), BF16),
            pltpu.SemaphoreType.DMA((4, 4)),
            pltpu.SemaphoreType.DMA((4, 4)),
            pltpu.SemaphoreType.DMA((2,)),
            pltpu.SemaphoreType.DMA((2,)),
            pltpu.SemaphoreType.DMA((2,)),
            pltpu.SemaphoreType.DMA((2,)),
            pltpu.SemaphoreType.DMA((2,)),
        ],
        compiler_params=pltpu.CompilerParams(
            collective_id=0, has_side_effects=True, vmem_limit_bytes=48 * 2**20
        ),
    )(*operands)

    def grid(x):
        return x.reshape(1, WLAT, WLON, LEV, C).transpose(0, 3, 1, 2, 4)

    gp_p, gp_s = lax.psum((gp_p.astype(BF16), gp_s.astype(BF16)), ("lat", "lon", "dp"))
    return grid(out_field), grid(out_grad), gp_p, gp_s


def solution(mesh):
    sizes = tuple(mesh.shape[a] for a in ("lat", "lon", "dp"))
    grid = P("dp", None, "lat", "lon", None)
    table = P(None, "lat", None, None)
    columns = P(None, "dp")
    return jax.shard_map(
        functools.partial(body, sizes),
        mesh=mesh,
        in_specs=(grid, grid, columns, P(), table, columns, P(), table),
        out_specs=(grid, grid, P(), P()),
        check_vma=False,
    )
```

time: 352 us -> 522 us (1.48)
  waiting for transfers between devices: 5.62 us -> 452 us
  blocking collectives: 138 us -> 0 us
  local copies, waits for them, and re-layouts: 109 us -> 13.3 us
  matrix products: 53.8 us -> 0 us
  Pallas kernels: 0 us -> 40.9 us
  starting transfers between devices: 24.5 us -> 0.04 us
  other arithmetic: 18.3 us -> 1.49 us
  between operations: 1.33 us -> 14.1 us
    psum x0 -> x1, waiting for transfers between devices: none -> 452 us  [body(): lax.psum((gp_p.astype(BF16), gp_s.astype(BF16)), ('lat', 'lon', 'dp'))]
    psum x1 -> x0, blocking collectives: 110 us -> none  [body(): lax.psum((grad_proj_a, grad_proj_b), ('lat', 'lon', 'dp'))]
    dot_general x24 -> x0, matrix products: 53.8 us -> none  [the longest x2 23.5 us: expand_bias(): jnp.einsum('nhabcdr,xyr->nhacxbdy', shaped, picker, preferred_element_typ...]
    pallas_call x0 -> x1, Pallas kernels: none -> 40.9 us  [body(): pl.pallas_call(functools.partial(kernel, sizes), out_shape=(grid_shape, g...]
    transpose x2 -> x0, local copies, waits for them, and re-layouts: 37.8 us -> none  [expand_bias(): jnp.einsum('nhabcdr,xyr->nhacxbdy', shaped, picker, preferred_element_typ...]
    another operation x10 -> x0, local copies, waits for them, and re-layouts: 34.9 us -> none  [the longest x2 25.3 us: body(): bias_a[None, :, None]]
    all_gather x2 -> x0, blocking collectives: 27.9 us -> none  [the longest x1 14 us: body(): lax.all_gather(qkv_plain, 'dp', axis=1, tiled=True)]
    reshape x2 -> x0, local copies, waits for them, and re-layouts: 25.3 us -> none  [expand_bias(): return full_bias.reshape(lev_n, HEADS, tokens, tokens)]
  transfers between devices with their start and end apart: 8 -> 1, of which waited for: 3 -> 1; matrix products, arithmetic and copies ran while one was open for 43% -> 0% of each run, Pallas kernels for 0% -> 0%
where the time goes in v1:
time: 522 us
  waiting for transfers between devices  452 us (87%)
  Pallas kernels  40.9 us (8%)
  between operations  14.1 us (3%)
  local copies, waits for them, and re-layouts  13.3 us (3%)
    psum x1, waiting for transfers between devices, body(): lax.psum((gp_p.astype(BF16), gp_s.astype(BF16)), ('lat', 'lon', 'dp'))  452 us
    pallas_call x1, Pallas kernels, body(): pl.pallas_call(functools.partial(kernel, sizes), out_shape=(grid_shape, g...  40.9 us
    unnamed x30, local copies, waits for them, and re-layouts  13.3 us
  transfers between devices with their start and end apart: 1, of which 1 were waited for; matrix products, arithmetic and copies ran while one was open for 0% of the time, Pallas kernels for 0%

profile of v1, /device:TPU:1, one launch (start us, length us, event | category | flops | bytes accessed | tf_op | source)
XLA Modules:
  0.0 521.7 jit_solution(3453349456714329796)
XLA Ops:
  7.2 0.0 all-reduce.3.cloned.1.call-start
  7.2 0.0 copy-start
  7.2 1.0 copy-done
  8.2 0.0 copy-start.1
  8.2 1.0 copy-done.1
  9.2 0.0 copy-start.2
  9.2 1.0 copy-done.2
  10.2 0.0 copy-start.3
  10.2 1.0 copy-done.3
  11.2 0.0 copy-start.4
  11.2 0.9 copy-done.4
  12.1 0.0 copy-start.5
  12.1 0.9 copy-done.5
  13.0 0.0 copy-start.6
  13.0 0.9 copy-done.6
  13.9 0.0 copy-start.7
  13.9 0.9 copy-done.7
  14.8 0.0 copy-start.8
  14.8 0.9 copy-done.8
  15.7 0.9 copy-done.9
  16.6 0.9 copy-done.10
  17.5 40.9 %shard_map.138 = (bf16[72,2,384]{2,1,0:T(2,128)(2,1)S(1)}, bf16[72,2,384]{2,1,0:T(2,128)(2,1)S(1)}, f32[384,384]{1,0:T(8,128)S(1)}, f32[384,384]{1,0:T(8,128)S(1)}) custom-call(bf16[72,2,384]{2,1,0:T(2,128)(2,1)S(1)} %bitcast.22, bf16[72,2,384]{2,1,0:T(2,128)(2,1)S(1)} %bitcast.23, bf16[576,384]{1,0:T(8,128)(2,1)S(1)} %bitcast.16, ...), custom_call_target="tpu_custom_call" | custom-call | tf_op jit(solution)/shard_map/pallas_call | solution.py:393
  58.4 0.7 convert_element_type.6
  59.1 0.7 convert_element_type.7
  59.9 0.0 all-reduce.3.cloned.1.call-update
  59.9 451.9 %all-reduce.3.cloned.1.call-done = (bf16[384,384]{1,0:T(8,128)(2,1)}, bf16[384,384]{1,0:T(8,128)(2,1)}) async-done(((bf16[384,384]{1,0:T(8,128)(2,1)}, bf16[384,384]{1,0:T(8,128)(2,1)}), (bf16[384,384]{1,0:T(8,128)(2,1)}, bf16[384,384]{1,0:T(8,128)(2,1)})) %all-reduce.3.cloned.1.call-update) | async-done | bytes 589840 | tf_op jit(solution)/shard_map/psum | solution.py:440
  511.8 0.6 copy.19
  512.4 0.6 copy.20
  513.1 0.0 copy-done.12
  513.1 0.7 copy.21
  513.8 0.4 copy-done.11
  514.1 0.7 copy.22
  (4 shorter events, 0.0 us)
Async XLA Ops:
  7.2 504.6 %all-reduce.3.cloned.1.call-start = ((), (), s32[]{:S(2)}) async-start(), calls=%async_computation | async-start | bytes 1179648 | tf_op jit(solution)/shard_map/psum | solution.py:440
  7.2 1.0 copy-start
  8.2 1.0 copy-start.1
  9.2 1.0 copy-start.2
  10.2 1.0 copy-start.3
  11.2 0.9 copy-start.4
  12.1 0.9 copy-start.5
  13.0 0.9 copy-start.6
  13.9 0.9 copy-start.7
  14.8 0.9 copy-start.8
  15.7 0.9 copy-start.9
  16.6 0.9 copy-start.10
  511.8 1.3 copy-start.12
  513.1 1.1 copy-start.11
Sparse Core Ops, SparseCore 0:
  60.0 451.7 all-reduce.2

commit v2 on v1

--- a/solution.py
+++ b/solution.py
@@ -56,19 +56,94 @@
     return gather, scatter, pick
 
 
-def kernel(
+OPERANDS = (
+    ("field", (WLAT * WLON, LEV, C)),
+    ("cot", (WLAT * WLON, LEV, C)),
+    ("wp_half", None),
+    ("ws_half", None),
+    ("tab_p", (HEADS, 4 * WLAT * CHUNK)),
+    ("tab_s", (HEADS, 4 * WLAT * CHUNK)),
+    ("scatter", (4 * QUAD, TOKENS)),
+    ("gather", (TOKENS, 4 * QUAD)),
+    ("pick", (TOKENS, 256)),
+    ("proj_p", (C, C)),
+    ("proj_s", (C, C)),
+)
+LOADED = [name for name, shape in OPERANDS if shape is not None]
+
+
+def scratch(plan):
+    xy, z, rows = plan
+    tokens_f32 = pltpu.VMEM((TOKENS, C), F32)
+    row_stat = pltpu.VMEM((TOKENS, 1), F32)
+    full_bias = pltpu.VMEM((HEADS, TOKENS, TOKENS), F32)
+    weights = pltpu.VMEM((2, 3 * C // 2, C), BF16)
+    qkv = pltpu.VMEM((TOKENS, 3 * C), BF16)
+    kvt = pltpu.VMEM((2 * C, TOKENS), BF16)
+    heads_t = pltpu.VMEM((C, TOKENS), BF16)
+    dma = pltpu.SemaphoreType.DMA
+    named = {name: pltpu.VMEM(shape, BF16) for name, shape in OPERANDS if shape is not None}
+    named |= dict(
+        load_sem=dma((len(OPERANDS),)),
+        wp=weights,
+        ws=weights,
+        xf=tokens_f32,
+        quads=pltpu.VMEM((4 * QUAD, C), F32),
+        xhat_p=tokens_f32,
+        rstd_p=row_stat,
+        xhat_s=tokens_f32,
+        rstd_s=row_stat,
+        s2f=tokens_f32,
+        dy2f=tokens_f32,
+        qkv_p=qkv,
+        kvt_p=kvt,
+        qkv_s=qkv,
+        kvt_s=kvt,
+        probs_p=full_bias,
+        probs_s=full_bias,
+        ot_p=heads_t,
+        ot_s=heads_t,
+        ot_r=heads_t,
+        dqkv=qkv,
+        dqt=pltpu.VMEM((C, TOKENS), F32),
+        bias_p=full_bias,
+        bias_s=full_bias,
+        tabf=pltpu.VMEM((16, 6400), F32),
+        spread=pltpu.VMEM((2, TOKENS * 16, 128), F32),
+        send=pltpu.VMEM((5, 4, QUAD, C), BF16),
+        recv=pltpu.VMEM((5, 4, QUAD, C), BF16),
+        halo_ss=dma((5, 4)),
+        halo_rs=dma((5, 4)),
+        w_ss=dma((2,)),
+        w_rs=dma((2,)),
+        f_ss=dma((2,)),
+        f_rs=dma((2,)),
+        part=pltpu.VMEM((2, C, C), F32),
+        part16=pltpu.VMEM((2, C, C), BF16),
+        half_in=pltpu.VMEM((2, C // 2, C), BF16),
+        chunks=pltpu.VMEM((2, C // 2 // rows, rows, C), BF16),
+        xy_in=pltpu.VMEM((2, xy, rows, C), BF16),
+        z_in=pltpu.VMEM((2, z, rows, C), BF16),
+        final=pltpu.VMEM((2, C // rows, rows, C), BF16),
+        c_ss=dma((2,)),
+        c_rs=dma((2,)),
+        xy_ss=dma((2, xy)),
+        xy_rs=dma((2, xy)),
+        z_ss=dma((2, z)),
+        z_rs=dma((2, z)),
+        fin_ss=dma((2, 2 * xy)),
+        fin_rs=dma((2, C // rows)),
+    )
+    return named
+
+
+def kernel(sizes, plan, names, *refs):
+    run(sizes, plan, **dict(zip(names, refs)))
+
+
+def run(
     sizes,
-    field,
-    cot,
-    wp_half,
-    ws_half,
-    proj_p,
-    proj_s,
-    tab_p,
-    tab_s,
-    gather,
-    scatter,
-    pick,
+    plan,
     out_field,
     out_grad,
     gp_p,
@@ -88,8 +163,10 @@
     qkv_s,
     kvt_s,
     probs_p,
+    probs_s,
     ot_p,
     ot_s,
+    ot_r,
     dqkv,
     dqt,
     bias_p,
@@ -100,11 +177,27 @@
     recv,
     halo_ss,
     halo_rs,
-    own_sem,
     w_ss,
     w_rs,
     f_ss,
     f_rs,
+    part,
+    part16,
+    half_in,
+    chunks,
+    xy_in,
+    z_in,
+    final,
+    c_ss,
+    c_rs,
+    xy_ss,
+    xy_rs,
+    z_ss,
+    z_rs,
+    fin_ss,
+    fin_rs,
+    load_sem,
+    **local,
 ):
     n_lat, n_lon, n_dp = sizes
     lat, lon, dp = lax.axis_index("lat"), lax.axis_index("lon"), lax.axis_index("dp")
@@ -119,18 +212,55 @@
             dp,
         )
 
-    greet = [sibling, across]
-    greet += [near(a, b) for a, b in ((1, 0), (0, 1), (1, 1), (-1, 0), (0, -1), (-1, -1))]
+    xy, n_z, chunk_rows = plan
+    n_y = n_lat // 2
+    n_own = C // 2 // chunk_rows
+    z = lax.rem(lon, n_z)
+    spot = (lon // n_z + 2 * dp) * n_y + lat // 2
+
+    def at_spot(e, c):
+        x = e // n_y
+        return (lax.rem(e, n_y) * 2 + c, lax.rem(x, 2) * n_z + z, x // 2)
+
+    def at_z(other):
+        return (lat, lon - z + other, dp)
+
+    def peer(d):
+        f = lax.rem(spot * 2 + core + d, 2 * xy)
+        return at_spot(f // 2, lax.rem(f, 2))
+
+    def each(n, do):
+        def step(d, carry):
+            do(d)
+            return carry
+
+        lax.fori_loop(1, n, step, 0)
+
     barrier = pltpu.get_barrier_semaphore()
-    for device in greet:
+
+    def greet(device):
         pl.semaphore_signal(barrier, inc=1, device_id=device, device_id_type=MESH)
-    own = [
-        pltpu.make_async_copy(wp_half, wp.at[dp], own_sem.at[0]),
-        pltpu.make_async_copy(ws_half, ws.at[dp], own_sem.at[1]),
-    ]
-    for copy in own:
-        copy.start()
-    pl.semaphore_wait(barrier, len(greet))
+
+    each(2 * xy, lambda d: greet(peer(d)))
+    around = [(0, 1), (1, 1), (0, -1), (-1, -1)]
+    for a, b in around:
+        greet(near(a, b))
+    each(n_z, lambda d: greet(at_z(lax.rem(z + d, n_z))))
+
+    loads = {}
+    for i, (name, shape) in enumerate(OPERANDS):
+        source = local[name + "_hbm"]
+        target = local[name] if shape else {"wp_half": wp, "ws_half": ws}[name].at[dp]
+        loads[name] = pltpu.make_async_copy(source, target, load_sem.at[i])
+        loads[name].start()
+    wp_half, ws_half = local["wp_half_hbm"], local["ws_half_hbm"]
+    field, cot, proj_p, proj_s, tab_p, tab_s, gather, scatter, pick = (
+        local[name]
+        for name in (
+            "field", "cot", "proj_p", "proj_s", "tab_p", "tab_s", "gather", "scatter", "pick"
+        )
+    )
+    pl.semaphore_wait(barrier, 2 * xy - 1 + len(around) + n_z - 1)
 
     rows = pl.ds(pl.multiple_of(core * 288, 32), 288)
 
@@ -186,6 +316,7 @@
     def to_quads(i, x):
         send[i] = nn(scatter[...], x).astype(BF16).reshape(4, QUAD, C)
 
+    loads["cot"].wait()
     quads[...] = jnp.zeros_like(quads)
     for h in range(WLAT):
         for w in range(WLON):
@@ -194,6 +325,7 @@
     send[0] = quads[...].astype(BF16).reshape(4, QUAD, C)
     halo_cot = halo(0, -1)
 
+    loads["field"].wait()
     for i in range(WLAT * WLON):
         xf[2 * i : 2 * i + 2, :] = field[i].astype(F32)
 
@@ -296,13 +428,123 @@
         product = jnp.mean(dn * xh, axis=-1, keepdims=True)
         return (dy + rstd[...] * (dn - mean - xh * product)).astype(BF16)
 
-    def output(x, ot, proj):
-        o = ot[...].astype(F32).T.astype(BF16)
+    def heads(ot):
+        return ot[...].astype(F32).T.astype(BF16)
+
+    def output(x, o, proj):
         return (x + nn(o, proj[...])).astype(BF16)
 
+    def copy_core(m):
+        return pltpu.make_async_remote_copy(
+            part16.at[m, pl.ds(pl.multiple_of((1 - core) * (C // 2), 64), C // 2)],
+            half_in.at[m],
+            c_ss.at[m],
+            c_rs.at[m],
+            device_id=sibling,
+            device_id_type=MESH,
+        )
+
+    def copy_xy(m, to, sender, ss):
+        return pltpu.make_async_remote_copy(
+            chunks.at[m, lax.rem(to, n_own)],
+            xy_in.at[m, sender],
+            xy_ss.at[m, ss],
+            xy_rs.at[m, sender],
+            device_id=at_spot(to, core),
+            device_id_type=MESH,
+        )
+
+    def copy_z(m, to, sender, ss):
+        return pltpu.make_async_remote_copy(
+            z_in.at[m, z],
+            z_in.at[m, sender],
+            z_ss.at[m, ss],
+            z_rs.at[m, sender],
+            device_id=at_z(to),
+            device_id_type=MESH,
+        )
+
+    def copy_final(m, d, index):
+        return pltpu.make_async_remote_copy(
+            final.at[m, index],
+            final.at[m, index],
+            fin_ss.at[m, d],
+            fin_rs.at[m, index],
+            device_id=peer(d),
+            device_id_type=MESH,
+        )
+
+    owner = spot < n_own
+    mine = core * n_own + lax.rem(spot, n_own)
+
+    def sum_start(m, total):
+        part[m] = total
+        part16[m] = total.astype(BF16)
+        copy_core(m).start()
+
+    def sum_xy(m):
+        copy_core(m).wait_recv()
+        at = pl.ds(pl.multiple_of(core * (C // 2), 64), C // 2)
+        both = part[m, at, :] + half_in[m].astype(F32)
+        chunks[m] = both.astype(BF16).reshape(n_own, chunk_rows, C)
+
+        def go(d):
+            to = lax.rem(spot + d, xy)
+
+            @pl.when(to < n_own)
+            def _():
+                copy_xy(m, to, spot, d).start()
+
+        each(xy, go)
+
+    def sum_z(m):
+        @pl.when(owner)
+        def _():
+            xy_in[m, spot] = chunks[m, spot]
+            each(xy, lambda d: copy_xy(m, spot, lax.rem(spot + d, xy), d).wait_recv())
+            z_in[m, z] = jnp.sum(xy_in[m].astype(F32), axis=0).astype(BF16)
+            each(n_z, lambda d: copy_z(m, lax.rem(z + d, n_z), z, d).start())
+
+    def sum_back(m):
+        @pl.when(owner)
+        def _():
+            each(n_z, lambda d: copy_z(m, z, lax.rem(z + d, n_z), d).wait_recv())
+            final[m, mine] = jnp.sum(z_in[m].astype(F32), axis=0).astype(BF16)
+            each(2 * xy, lambda d: copy_final(m, d, mine).start())
+
+    def sum_end(m, out):
+        def take(i, carry):
+            @pl.when(jnp.logical_not(owner & (i == mine)))
+            def _():
+                copy_final(m, 1, i).wait_recv()
+
+            return carry
+
+        lax.fori_loop(0, C // chunk_rows, take, 0)
+        out[...] = final[m].reshape(C, C)
+
+    def sum_sent(m):
+        copy_core(m).wait_send()
+
+        def sent(d):
+            to = lax.rem(spot + d, xy)
+
+            @pl.when(to < n_own)
+            def _():
+                copy_xy(m, to, spot, d).wait_send()
+
+        each(xy, sent)
+
+        @pl.when(owner)
+        def _():
+            each(n_z, lambda d: copy_z(m, lax.rem(z + d, n_z), z, d).wait_send())
+            each(2 * xy, lambda d: copy_final(m, d, mine).wait_send())
+
     n1 = norm(xf[...], xhat_p, rstd_p)
+    loads["tab_p"].wait()
+    loads["pick"].wait()
     expand(tab_p, bias_p, None)
-    own[0].wait()
+    loads["wp_half"].wait()
     first[0].wait_recv()
     beside[0].start()
     beside[0].wait_recv()
@@ -311,20 +553,27 @@
         p = softmax(g, qkv_p, bias_p)
         probs_p[g * PER : (g + 1) * PER] = p
         values(g, p.astype(BF16), kvt_p, ot_p)
-    h1 = output(xf[...], ot_p, proj_p)
-    to_quads(1, h1)
+    loads["proj_p"].wait()
+    loads["scatter"].wait()
+    o1 = heads(ot_p)
+    to_quads(1, output(xf[...], o1, proj_p))
     halo_h1 = halo(1, -1)
+    to_quads(4, o1)
+    halo_o1 = halo(4, -1)
 
     key = lax.broadcasted_iota(jnp.int32, (TOKENS, TOKENS), 0)
     query = lax.broadcasted_iota(jnp.int32, (TOKENS, TOKENS), 1)
     edge = jnp.where(lat == n_lat - 1, TOKENS // 2, TOKENS)
     same = ((key & 1) == (query & 1)) & ((key >= edge) == (query >= edge))
+    loads["tab_s"].wait()
     expand(tab_s, bias_s, jnp.where(same, 0.0, -1e30))
-    own[1].wait()
+    loads["ws_half"].wait()
     first[1].wait_recv()
     beside[1].start()
+    loads["gather"].wait()
     dy2 = arrived(0, halo_cot)
     dy2f[...] = dy2
+    loads["proj_s"].wait()
     do2 = nt(dy2.astype(BF16), proj_s[...]).astype(BF16)
     beside[1].wait_recv()
 
@@ -334,35 +583,48 @@
     project(n2, ws, qkv_s, kvt_s)
     for g in range(GROUPS):
         p = softmax(g, qkv_s, bias_s)
-        pb = p.astype(BF16)
-        values(g, pb, kvt_s, ot_s)
-        grads(g, p, pb, do2, qkv_s, kvt_s)
+        probs_s[g * PER : (g + 1) * PER] = p
+        values(g, p.astype(BF16), kvt_s, ot_s)
+    sum_start(1, nn(ot_s[...], dy2f[...].astype(BF16)))
+    for g in range(GROUPS):
+        p = probs_s[g * PER : (g + 1) * PER]
+        grads(g, p, p.astype(BF16), do2, qkv_s, kvt_s)
+        if g == 0:
+            sum_xy(1)
+            ot_r[...] = arrived(4, halo_o1).T.astype(BF16)
     ds2 = input_grad(dy2f[...], ws, xhat_s, rstd_s)
+    sum_start(0, nn(ot_r[...], ds2))
     to_quads(2, ds2)
     halo_g1 = halo(2, 1)
 
-    y2 = output(s2f[...], ot_s, proj_s)
+    y2 = output(s2f[...], heads(ot_s), proj_s)
     to_quads(3, y2)
     halo_out = halo(3, 1)
-    gp_s[...] = nn(ot_s[...], dy2f[...].astype(BF16))
+    sum_xy(0)
+    sum_z(1)
 
     g1 = arrived(2, halo_g1)
-    g1b = g1.astype(BF16)
-    gp_p[...] = nn(ot_p[...], g1b)
-    do1 = nt(g1b, proj_p[...]).astype(BF16)
+    do1 = nt(g1.astype(BF16), proj_p[...]).astype(BF16)
     for g in range(GROUPS):
         p = probs_p[g * PER : (g + 1) * PER]
         grads(g, p, p.astype(BF16), do1, qkv_p, kvt_p)
+        if g == 1:
+            sum_z(0)
     xf[...] = input_grad(g1, wp, xhat_p, rstd_p).astype(F32)
     for i in range(WLAT * WLON):
         out_grad[i] = xf[2 * i : 2 * i + 2, :].astype(BF16)
     s2f[...] = arrived(3, halo_out)
     for i in range(WLAT * WLON):
         out_field[i] = s2f[2 * i : 2 * i + 2, :].astype(BF16)
-
-    for copies in (halo_cot, halo_h1, halo_g1, halo_out, first, beside):
+    sum_back(1)
+    sum_back(0)
+    for copies in (halo_cot, halo_h1, halo_o1, halo_g1, halo_out, first, beside):
         for copy in copies:
             copy.wait_send()
+    sum_end(1, gp_s)
+    sum_end(0, gp_p)
+    sum_sent(1)
+    sum_sent(0)
 
 
 def body(sizes, field, cotangent, qkv_plain, proj_plain, bias_plain, qkv_shift, proj_shift, bias_shift):
@@ -370,74 +632,44 @@
         return x.transpose(0, 2, 3, 1, 4).reshape(WLAT * WLON, LEV, C)
 
     gather, scatter, pick = constants()
-    operands = (
-        rows(field),
-        rows(cotangent),
-        qkv_plain.T,
-        qkv_shift.T,
-        proj_plain,
-        proj_shift,
-        bias_plain.reshape(HEADS, -1),
-        bias_shift.reshape(HEADS, -1),
-        jnp.asarray(gather, BF16),
-        jnp.asarray(scatter, BF16),
-        jnp.asarray(pick, BF16),
+    operands = dict(
+        field=rows(field),
+        cot=rows(cotangent),
+        wp_half=qkv_plain.T,
+        ws_half=qkv_shift.T,
+        proj_p=proj_plain,
+        proj_s=proj_shift,
+        tab_p=bias_plain.reshape(HEADS, -1),
+        tab_s=bias_shift.reshape(HEADS, -1),
+        gather=jnp.asarray(gather, BF16),
+        scatter=jnp.asarray(scatter, BF16),
+        pick=jnp.asarray(pick, BF16),
     )
+    n_lat, n_lon, n_dp = sizes
+    xy = n_lat // 2 * 2 * n_dp
+    owners = max(d for d in (1, 2, 3, 4, 6, 12) if d <= xy)
+    plan = (xy, n_lon // 2, C // 2 // owners)
+    buffers = scratch(plan)
     vmem = pl.BlockSpec(memory_space=pltpu.VMEM)
     hbm = pl.BlockSpec(memory_space=pl.ANY)
     grid_shape = jax.ShapeDtypeStruct((WLAT * WLON, LEV, C), BF16)
-    square = jax.ShapeDtypeStruct((C, C), F32)
-    tokens_f32 = pltpu.VMEM((TOKENS, C), F32)
-    row_stat = pltpu.VMEM((TOKENS, 1), F32)
-    full_bias = pltpu.VMEM((HEADS, TOKENS, TOKENS), F32)
+    square = jax.ShapeDtypeStruct((C, C), BF16)
+    names = [name + "_hbm" for name, _ in OPERANDS]
+    names += ["out_field", "out_grad", "gp_p", "gp_s"] + list(buffers)
     out_field, out_grad, gp_p, gp_s = pl.pallas_call(
-        functools.partial(kernel, sizes),
+        functools.partial(kernel, sizes, plan, names),
         out_shape=(grid_shape, grid_shape, square, square),
-        in_specs=[vmem, vmem, hbm, hbm] + [vmem] * 7,
+        in_specs=[hbm] * len(OPERANDS),
         out_specs=(vmem, vmem, vmem, vmem),
-        scratch_shapes=[
-            pltpu.VMEM((2, 3 * C // 2, C), BF16),
-            pltpu.VMEM((2, 3 * C // 2, C), BF16),
-            tokens_f32,
-            pltpu.VMEM((4 * QUAD, C), F32),
-            tokens_f32,
-            row_stat,
-            tokens_f32,
-            row_stat,
-            tokens_f32,
-            tokens_f32,
-            pltpu.VMEM((TOKENS, 3 * C), BF16),
-            pltpu.VMEM((2 * C, TOKENS), BF16),
-            pltpu.VMEM((TOKENS, 3 * C), BF16),
-            pltpu.VMEM((2 * C, TOKENS), BF16),
-            full_bias,
-            pltpu.VMEM((C, TOKENS), BF16),
-            pltpu.VMEM((C, TOKENS), BF16),
-            pltpu.VMEM((TOKENS, 3 * C), BF16),
-            pltpu.VMEM((C, TOKENS), F32),
-            full_bias,
-            full_bias,
-            pltpu.VMEM((16, 6400), F32),
-            pltpu.VMEM((2, TOKENS * 16, 128), F32),
-            pltpu.VMEM((4, 4, QUAD, C), BF16),
-            pltpu.VMEM((4, 4, QUAD, C), BF16),
-            pltpu.SemaphoreType.DMA((4, 4)),
-            pltpu.SemaphoreType.DMA((4, 4)),
-            pltpu.SemaphoreType.DMA((2,)),
-            pltpu.SemaphoreType.DMA((2,)),
-            pltpu.SemaphoreType.DMA((2,)),
-            pltpu.SemaphoreType.DMA((2,)),
-            pltpu.SemaphoreType.DMA((2,)),
-        ],
+        scratch_shapes=list(buffers.values()),
         compiler_params=pltpu.CompilerParams(
-            collective_id=0, has_side_effects=True, vmem_limit_bytes=48 * 2**20
+            collective_id=0, has_side_effects=True, vmem_limit_bytes=56 * 2**20
         ),
-    )(*operands)
+    )(*[operands[name] for name, _ in OPERANDS])
 
     def grid(x):
         return x.reshape(1, WLAT, WLON, LEV, C).transpose(0, 3, 1, 2, 4)
 
-    gp_p, gp_s = lax.psum((gp_p.astype(BF16), gp_s.astype(BF16)), ("lat", "lon", "dp"))
     return grid(out_field), grid(out_grad), gp_p, gp_s
 
 

time: 522 us -> 80.1 us (0.15)
  waiting for transfers between devices: 452 us -> 0 us
  Pallas kernels: 40.9 us -> 74.2 us
  between operations: 14.1 us -> 0.65 us
  local copies, waits for them, and re-layouts: 13.3 us -> 5.07 us
    psum x1 -> x0, waiting for transfers between devices: 452 us -> none  [body(): lax.psum((gp_p.astype(BF16), gp_s.astype(BF16)), ('lat', 'lon', 'dp'))]
    pallas_call x1, Pallas kernels: 40.9 us -> 74.2 us  [body(): pl.pallas_call(functools.partial(kernel, sizes, plan, names), out_shape=(...]
    unnamed x30 -> x8, local copies, waits for them, and re-layouts: 13.3 us -> 5.07 us
  transfers between devices with their start and end apart: 1 -> 0, of which waited for: 1 -> 0; matrix products, arithmetic and copies ran while one was open for 0% -> 0% of each run, Pallas kernels for 0% -> 0%
where the time goes in v2:
time: 80.1 us; the launch traced here: 79.9 us
  Pallas kernels  74.2 us (93%)
  local copies, waits for them, and re-layouts  5.07 us (6%)
    pallas_call x1, Pallas kernels, body(): pl.pallas_call(functools.partial(kernel, sizes, plan, names), out_shape=(...  74.2 us
    unnamed x8, local copies, waits for them, and re-layouts  5.07 us

profile of v2, /device:TPU:1, one launch (start us, length us, event | category | flops | bytes accessed | tf_op | source)
XLA Modules:
  0.0 79.9 jit_solution(12756005268246030268)
XLA Ops:
  0.6 74.2 %shard_map.138 = (bf16[72,2,384]{2,1,0:T(2,128)(2,1)}, bf16[72,2,384]{2,1,0:T(2,128)(2,1)}, bf16[384,384]{1,0:T(8,128)(2,1)}, bf16[384,384]{1,0:T(8,128)(2,1)}) custom-call(bf16[72,2,384]{2,1,0:T(2,128)(2,1)} %bitcast.22, bf16[72,2,384]{2,1,0:T(2,128)(2,1)} %bitcast.23, bf16[576,384]{1,0:T(8,128)(2,1)} %bitcast.16, bf16[576,384]{1,0:T(8,128)(2,1)} %bitcast.17, ...), custom_call_target="tpu_custom_call" | custom-call | tf_op jit(solution)/shard_map/pallas_call | solution.py:659
  74.8 0.0 copy-start.1
  74.8 1.7 %copy.19 = bf16[1,2,12,6,384]{4,1,3,2,0:T(2,128)(2,1)} copy(bf16[1,2,12,6,384]{4,1,3,2,0:T(2,128)(2,1)} %bitcast.21) | data formatting | bytes 221184
  76.5 1.6 %copy.20 = bf16[1,2,12,6,384]{4,1,3,2,0:T(2,128)(2,1)} copy(bf16[1,2,12,6,384]{4,1,3,2,0:T(2,128)(2,1)} %bitcast.20) | data formatting | bytes 221184
  78.1 0.0 copy-done.1
  78.1 0.0 copy-start
  78.1 0.7 copy.21
  78.8 0.4 copy-done
  79.2 0.7 copy.22
Async XLA Ops:
  74.8 3.3 %copy-start.1 = (bf16[384,384]{1,0:T(8,128)(2,1)S(1)}, bf16[384,384]{1,0:T(8,128)(2,1)}, u32[]{:S(2)}) copy-start(bf16[384,384]{1,0:T(8,128)(2,1)} %get-tuple-element.18) | copy-start | bytes 884740
  78.1 1.1 %copy-start = (bf16[384,384]{1,0:T(8,128)(2,1)S(1)}, bf16[384,384]{1,0:T(8,128)(2,1)}, u32[]{:S(2)}) copy-start(bf16[384,384]{1,0:T(8,128)(2,1)} %get-tuple-element.19) | copy-start | bytes 884740

commit v3 on v2

--- a/solution.py
+++ b/solution.py
@@ -124,7 +124,10 @@
         chunks=pltpu.VMEM((2, C // 2 // rows, rows, C), BF16),
         xy_in=pltpu.VMEM((2, xy, rows, C), BF16),
         z_in=pltpu.VMEM((2, z, rows, C), BF16),
-        final=pltpu.VMEM((2, C // rows, rows, C), BF16),
+        final=pltpu.VMEM((2, C, C), BF16),
+        out_sem=dma((4,)),
+        field_out=pltpu.VMEM((WLAT * WLON, LEV, C), BF16),
+        grad_out=pltpu.VMEM((WLAT * WLON, LEV, C), BF16),
         c_ss=dma((2,)),
         c_rs=dma((2,)),
         xy_ss=dma((2, xy)),
@@ -132,6 +135,7 @@
         z_ss=dma((2, z)),
         z_rs=dma((2, z)),
         fin_ss=dma((2, 2 * xy)),
+        roll=pltpu.SemaphoreType.REGULAR((3,)),
         fin_rs=dma((2, C // rows)),
     )
     return named
@@ -196,7 +200,11 @@
     z_rs,
     fin_ss,
     fin_rs,
+    roll,
     load_sem,
+    out_sem,
+    field_out,
+    grad_out,
     **local,
 ):
     n_lat, n_lon, n_dp = sizes
@@ -225,10 +233,6 @@
     def at_z(other):
         return (lat, lon - z + other, dp)
 
-    def peer(d):
-        f = lax.rem(spot * 2 + core + d, 2 * xy)
-        return at_spot(f // 2, lax.rem(f, 2))
-
     def each(n, do):
         def step(d, carry):
             do(d)
@@ -236,17 +240,35 @@
 
         lax.fori_loop(1, n, step, 0)
 
+    def greet(semaphore, device):
+        pl.semaphore_signal(semaphore, inc=1, device_id=device, device_id_type=MESH)
+
+    def along_z(d):
+        return (lat, lon - z + lax.rem(z + d + 8 * n_z, n_z), dp)
+
+    beside_x = (lat, across[1], dp)
+    y_up, y_down = near(2, 0), near(-2, 0)
     barrier = pltpu.get_barrier_semaphore()
-
-    def greet(device):
-        pl.semaphore_signal(barrier, inc=1, device_id=device, device_id_type=MESH)
-
-    each(2 * xy, lambda d: greet(peer(d)))
-    around = [(0, 1), (1, 1), (0, -1), (-1, -1)]
-    for a, b in around:
-        greet(near(a, b))
-    each(n_z, lambda d: greet(at_z(lax.rem(z + d, n_z))))
-
+    around = [across, sibling, beside_x, y_up, y_down, along_z(1), along_z(-1)]
+    around += [near(a, b) for a, b in ((1, 0), (-1, 0), (0, 1), (0, -1), (1, 1), (-1, -1))]
+    for device in around:
+        greet(barrier, device)
+
+    def tell(i):
+        for device in (across, sibling, beside_x, y_up, y_down):
+            greet(roll.at[i], device)
+        for d in (2**i, -(2**i)):
+            greet(roll.at[i], along_z(d))
+
+    def told(i):
+        pl.semaphore_wait(roll.at[i], 7)
+
+    results = [
+        pltpu.make_async_copy(a, b, out_sem.at[i])
+        for i, (a, b) in enumerate(
+            ((final.at[0], gp_p), (final.at[1], gp_s), (field_out, out_field), (grad_out, out_grad))
+        )
+    ]
     loads = {}
     for i, (name, shape) in enumerate(OPERANDS):
         source = local[name + "_hbm"]
@@ -260,7 +282,7 @@
             "field", "cot", "proj_p", "proj_s", "tab_p", "tab_s", "gather", "scatter", "pick"
         )
     )
-    pl.semaphore_wait(barrier, 2 * xy - 1 + len(around) + n_z - 1)
+    pl.semaphore_wait(barrier, len(around))
 
     rows = pl.ds(pl.multiple_of(core * 288, 32), 288)
 
@@ -281,8 +303,7 @@
         )
 
     first = [weights_across(wp_half, wp, 0), weights_across(ws_half, ws, 1)]
-    for copy in first:
-        copy.start()
+    first[0].start()
     beside = [weights_beside(wp, 0), weights_beside(ws, 1)]
 
     def halo(i, by):
@@ -324,6 +345,7 @@
             quads[at : at + 2, :] = cot[h * WLON + w].astype(F32)
     send[0] = quads[...].astype(BF16).reshape(4, QUAD, C)
     halo_cot = halo(0, -1)
+    tell(0)
 
     loads["field"].wait()
     for i in range(WLAT * WLON):
@@ -444,9 +466,12 @@
             device_id_type=MESH,
         )
 
+    def owned(m, e):
+        return lax.rem(e + xy - m * n_y, xy)
+
     def copy_xy(m, to, sender, ss):
         return pltpu.make_async_remote_copy(
-            chunks.at[m, lax.rem(to, n_own)],
+            chunks.at[m, lax.rem(owned(m, to), n_own)],
             xy_in.at[m, sender],
             xy_ss.at[m, ss],
             xy_rs.at[m, sender],
@@ -464,18 +489,31 @@
             device_id_type=MESH,
         )
 
-    def copy_final(m, d, index):
+    def chunk(index):
+        return pl.ds(pl.multiple_of(index * chunk_rows, 16), chunk_rows)
+
+    def copy_final(m, index, ss, device):
         return pltpu.make_async_remote_copy(
-            final.at[m, index],
-            final.at[m, index],
-            fin_ss.at[m, d],
+            final.at[m, chunk(index)],
+            final.at[m, chunk(index)],
+            fin_ss.at[m, ss],
             fin_rs.at[m, index],
-            device_id=peer(d),
+            device_id=device,
             device_id_type=MESH,
         )
 
-    owner = spot < n_own
-    mine = core * n_own + lax.rem(spot, n_own)
+    def copy_spread(m, d):
+        device = at_spot(lax.rem(spot + d, xy), core)
+        return copy_final(m, core * n_own + lax.rem(owned(m, spot), n_own), d, device)
+
+    def copy_beside(m, i):
+        return copy_final(m, core * n_own + i, xy + i, sibling)
+
+    def far_first(k):
+        return n_z // 2 + (2 * lax.rem(k, 2) - 1) * (k // 2)
+
+    def if_owner(m):
+        return pl.when(owned(m, spot) < n_own)
 
     def sum_start(m, total):
         part[m] = total
@@ -491,37 +529,54 @@
         def go(d):
             to = lax.rem(spot + d, xy)
 
-            @pl.when(to < n_own)
+            @if_owner_of(m, to)
             def _():
                 copy_xy(m, to, spot, d).start()
 
         each(xy, go)
 
+    def if_owner_of(m, e):
+        return pl.when(owned(m, e) < n_own)
+
     def sum_z(m):
-        @pl.when(owner)
+        @if_owner(m)
         def _():
-            xy_in[m, spot] = chunks[m, spot]
+            xy_in[m, spot] = chunks[m, lax.rem(owned(m, spot), n_own)]
             each(xy, lambda d: copy_xy(m, spot, lax.rem(spot + d, xy), d).wait_recv())
             z_in[m, z] = jnp.sum(xy_in[m].astype(F32), axis=0).astype(BF16)
-            each(n_z, lambda d: copy_z(m, lax.rem(z + d, n_z), z, d).start())
+
+            def go(k):
+                d = far_first(k)
+                copy_z(m, lax.rem(z + d, n_z), z, d).start()
+
+            each(n_z, go)
 
     def sum_back(m):
-        @pl.when(owner)
+        @if_owner(m)
         def _():
             each(n_z, lambda d: copy_z(m, z, lax.rem(z + d, n_z), d).wait_recv())
-            final[m, mine] = jnp.sum(z_in[m].astype(F32), axis=0).astype(BF16)
-            each(2 * xy, lambda d: copy_final(m, d, mine).start())
-
-    def sum_end(m, out):
+            index = core * n_own + lax.rem(owned(m, spot), n_own)
+            final[m, chunk(index), :] = jnp.sum(z_in[m].astype(F32), axis=0).astype(BF16)
+            each(xy, lambda d: copy_spread(m, d).start())
+
+    def sum_share(m):
         def take(i, carry):
-            @pl.when(jnp.logical_not(owner & (i == mine)))
+            @pl.when(owned(m, spot) != i)
             def _():
-                copy_final(m, 1, i).wait_recv()
-
+                copy_final(m, core * n_own + i, 0, sibling).wait_recv()
+
+            copy_beside(m, i).start()
             return carry
 
-        lax.fori_loop(0, C // chunk_rows, take, 0)
-        out[...] = final[m].reshape(C, C)
+        lax.fori_loop(0, n_own, take, 0)
+
+    def sum_end(m):
+        def take(i, carry):
+            copy_final(m, (1 - core) * n_own + i, 0, sibling).wait_recv()
+            return carry
+
+        lax.fori_loop(0, n_own, take, 0)
+        results[m].start()
 
     def sum_sent(m):
         copy_core(m).wait_send()
@@ -529,21 +584,31 @@
         def sent(d):
             to = lax.rem(spot + d, xy)
 
-            @pl.when(to < n_own)
+            @if_owner_of(m, to)
             def _():
                 copy_xy(m, to, spot, d).wait_send()
 
         each(xy, sent)
 
-        @pl.when(owner)
+        @if_owner(m)
         def _():
             each(n_z, lambda d: copy_z(m, lax.rem(z + d, n_z), z, d).wait_send())
-            each(2 * xy, lambda d: copy_final(m, d, mine).wait_send())
+            each(xy, lambda d: copy_spread(m, d).wait_send())
+
+        def passed(i, carry):
+            copy_beside(m, i).wait_send()
+            return carry
+
+        lax.fori_loop(0, n_own, passed, 0)
 
     n1 = norm(xf[...], xhat_p, rstd_p)
     loads["tab_p"].wait()
     loads["pick"].wait()
     expand(tab_p, bias_p, None)
+    first[0].wait_send()
+    first[1].start()
+    told(0)
+    tell(1)
     loads["wp_half"].wait()
     first[0].wait_recv()
     beside[0].start()
@@ -560,6 +625,8 @@
     halo_h1 = halo(1, -1)
     to_quads(4, o1)
     halo_o1 = halo(4, -1)
+    told(1)
+    tell(2)
 
     key = lax.broadcasted_iota(jnp.int32, (TOKENS, TOKENS), 0)
     query = lax.broadcasted_iota(jnp.int32, (TOKENS, TOKENS), 1)
@@ -576,6 +643,7 @@
     loads["proj_s"].wait()
     do2 = nt(dy2.astype(BF16), proj_s[...]).astype(BF16)
     beside[1].wait_recv()
+    told(2)
 
     s2 = arrived(1, halo_h1)
     s2f[...] = s2
@@ -612,19 +680,38 @@
             sum_z(0)
     xf[...] = input_grad(g1, wp, xhat_p, rstd_p).astype(F32)
     for i in range(WLAT * WLON):
-        out_grad[i] = xf[2 * i : 2 * i + 2, :].astype(BF16)
+        grad_out[i] = xf[2 * i : 2 * i + 2, :].astype(BF16)
+    results[3].start()
     s2f[...] = arrived(3, halo_out)
     for i in range(WLAT * WLON):
-        out_field[i] = s2f[2 * i : 2 * i + 2, :].astype(BF16)
+        field_out[i] = s2f[2 * i : 2 * i + 2, :].astype(BF16)
+    results[2].start()
     sum_back(1)
     sum_back(0)
-    for copies in (halo_cot, halo_h1, halo_o1, halo_g1, halo_out, first, beside):
+    for copies in (halo_cot, halo_h1, halo_o1, halo_g1, halo_out, first[1:], beside):
         for copy in copies:
             copy.wait_send()
-    sum_end(1, gp_s)
-    sum_end(0, gp_p)
+    sum_share(1)
+    sum_share(0)
+    sum_end(1)
+    sum_end(0)
     sum_sent(1)
     sum_sent(0)
+    for copy in results:
+        copy.wait()
+
+
+def store(*refs):
+    sources, targets, staged, semaphores = refs[:4], refs[4:8], refs[8:12], refs[12]
+    taken = [pltpu.make_async_copy(sources[i], staged[i], semaphores.at[i]) for i in range(4)]
+    given = [pltpu.make_async_copy(staged[i], targets[i], semaphores.at[4 + i]) for i in range(4)]
+    for copy in taken:
+        copy.start()
+    for before, after in zip(taken, given):
+        before.wait()
+        after.start()
+    for copy in given:
+        copy.wait()
 
 
 def body(sizes, field, cotangent, qkv_plain, proj_plain, bias_plain, qkv_shift, proj_shift, bias_shift):
@@ -650,7 +737,6 @@
     owners = max(d for d in (1, 2, 3, 4, 6, 12) if d <= xy)
     plan = (xy, n_lon // 2, C // 2 // owners)
     buffers = scratch(plan)
-    vmem = pl.BlockSpec(memory_space=pltpu.VMEM)
     hbm = pl.BlockSpec(memory_space=pl.ANY)
     grid_shape = jax.ShapeDtypeStruct((WLAT * WLON, LEV, C), BF16)
     square = jax.ShapeDtypeStruct((C, C), BF16)
@@ -660,12 +746,23 @@
         functools.partial(kernel, sizes, plan, names),
         out_shape=(grid_shape, grid_shape, square, square),
         in_specs=[hbm] * len(OPERANDS),
-        out_specs=(vmem, vmem, vmem, vmem),
+        out_specs=[hbm] * 4,
         scratch_shapes=list(buffers.values()),
         compiler_params=pltpu.CompilerParams(
             collective_id=0, has_side_effects=True, vmem_limit_bytes=56 * 2**20
         ),
     )(*[operands[name] for name, _ in OPERANDS])
+
+    results = (out_field, out_grad, gp_p, gp_s)
+    out_field, out_grad, gp_p, gp_s = pl.pallas_call(
+        store,
+        out_shape=tuple(jax.ShapeDtypeStruct(x.shape, x.dtype) for x in results),
+        in_specs=[hbm] * 4,
+        out_specs=[hbm] * 4,
+        scratch_shapes=[pltpu.VMEM(x.shape, x.dtype) for x in results]
+        + [pltpu.SemaphoreType.DMA((8,))],
+        compiler_params=pltpu.CompilerParams(vmem_limit_bytes=56 * 2**20),
+    )(*results)
 
     def grid(x):
         return x.reshape(1, WLAT, WLON, LEV, C).transpose(0, 3, 1, 2, 4)

time: 80.1 us -> 71.2 us (0.89)
  local copies, waits for them, and re-layouts: 5.07 us -> 0 us
  Pallas kernels: 74.2 us -> 70.4 us
    pallas_call x1, Pallas kernels: 74.2 us -> 68.5 us  [body(): pl.pallas_call(functools.partial(kernel, sizes, plan, names), out_shape=(...]
    unnamed x8 -> x0, local copies, waits for them, and re-layouts: 5.07 us -> none
    pallas_call x0 -> x1, Pallas kernels: none -> 1.96 us  [body(): pl.pallas_call(store, out_shape=tuple((jax.ShapeDtypeStruct(x.shape, x.dt...]
where the time goes in v3:
time: 71.2 us; the launch traced here: 71.1 us
  Pallas kernels  70.4 us (99%)
    pallas_call x1, Pallas kernels, body(): pl.pallas_call(functools.partial(kernel, sizes, plan, names), out_shape=(...  68.5 us
    pallas_call x1, Pallas kernels, body(): pl.pallas_call(store, out_shape=tuple((jax.ShapeDtypeStruct(x.shape, x.dt...  1.96 us

profile of v3, /device:TPU:1, one launch (start us, length us, event | category | flops | bytes accessed | tf_op | source)
XLA Modules:
  0.0 71.1 jit_solution(18128062525795749782)
XLA Ops:
  0.6 68.5 %shard_map.138 = (bf16[72,2,384]{2,1,0:T(2,128)(2,1)}, bf16[72,2,384]{2,1,0:T(2,128)(2,1)}, bf16[384,384]{1,0:T(8,128)(2,1)}, bf16[384,384]{1,0:T(8,128)(2,1)}) custom-call(bf16[72,2,384]{2,1,0:T(2,128)(2,1)} %bitcast.20, bf16[72,2,384]{2,1,0:T(2,128)(2,1)} %bitcast.21, bf16[576,384]{1,0:T(8,128)(2,1)} %bitcast.16, bf16[576,384]{1,0:T(8,128)(2,1)} %bitcast.17, ...), custom_call_target="tpu_custom_call" | custom-call | tf_op jit(solution)/shard_map/pallas_call | solution.py:745
  69.1 2.0 %shard_map.139 = (bf16[72,2,384]{2,1,0:T(2,128)(2,1)}, bf16[72,2,384]{2,1,0:T(2,128)(2,1)}, bf16[384,384]{1,0:T(8,128)(2,1)}, bf16[384,384]{1,0:T(8,128)(2,1)}) custom-call(bf16[72,2,384]{2,1,0:T(2,128)(2,1)} %get-tuple-element.12.refs_0_, bf16[72,2,384]{2,1,0:T(2,128)(2,1)} %get-tuple-element.13.refs_1_, bf16[384,384]{1,0:T(8,128)(2,1)} %get-tuple-element.14.refs_2_, ...), custom_call_target="tpu_custom_call" | custom-call | tf_op jit(solution)/shard_map/pallas_call | solution.py:757

commit v4 on v3

--- a/solution.py
+++ b/solution.py
@@ -130,13 +130,15 @@
         grad_out=pltpu.VMEM((WLAT * WLON, LEV, C), BF16),
         c_ss=dma((2,)),
         c_rs=dma((2,)),
-        xy_ss=dma((2, xy)),
-        xy_rs=dma((2, xy)),
-        z_ss=dma((2, z)),
-        z_rs=dma((2, z)),
-        fin_ss=dma((2, 2 * xy)),
+        xy_ss=dma((2,)),
+        xy_rs=dma((2,)),
+        z_ss=dma((2, 2)),
+        z_rs=dma((2, 2)),
+        fin_ss=dma((2,)),
+        fin_rs=dma((2,)),
+        half_ss=dma((2,)),
+        half_rs=dma((2,)),
         roll=pltpu.SemaphoreType.REGULAR((3,)),
-        fin_rs=dma((2, C // rows)),
     )
     return named
 
@@ -200,6 +202,8 @@
     z_rs,
     fin_ss,
     fin_rs,
+    half_ss,
+    half_rs,
     roll,
     load_sem,
     out_sem,
@@ -224,21 +228,29 @@
     n_y = n_lat // 2
     n_own = C // 2 // chunk_rows
     z = lax.rem(lon, n_z)
-    spot = (lon // n_z + 2 * dp) * n_y + lat // 2
-
-    def at_spot(e, c):
-        x = e // n_y
-        return (lax.rem(e, n_y) * 2 + c, lax.rem(x, 2) * n_z + z, x // 2)
-
-    def at_z(other):
-        return (lat, lon - z + other, dp)
-
-    def each(n, do):
-        def step(d, carry):
-            do(d)
-            return carry
-
-        lax.fori_loop(1, n, step, 0)
+    x_lo, row = lax.div(lon, n_z), lax.div(lat, 2)
+
+    def wrap(value, size):
+        return jnp.where(value >= size, value - size, value)
+
+    def place(move):
+        lo, hi, up = move
+        to_lo = 1 - x_lo if lo else x_lo
+        to_hi = 1 - dp if hi else dp
+        to_row = wrap(row + up, n_y)
+        device = (2 * to_row + core, to_lo * n_z + z, to_hi)
+        return (to_lo + 2 * to_hi) * n_y + to_row, device
+
+    def hops(move):
+        lo, hi, up = move
+        return (1 if lo else 2 * hi) + min(up, n_y - up)
+
+    moves = [(lo, hi, up) for lo in range(2) for hi in range(2) for up in range(n_y)][1:]
+    moves = sorted(moves, key=hops, reverse=True)
+    spot = place((0, 0, 0))[0]
+
+    def at_z(d):
+        return (lat, lon - z + wrap(z + d, n_z), dp)
 
     def greet(semaphore, device):
         pl.semaphore_signal(semaphore, inc=1, device_id=device, device_id_type=MESH)
@@ -458,7 +470,7 @@
 
     def copy_core(m):
         return pltpu.make_async_remote_copy(
-            part16.at[m, pl.ds(pl.multiple_of((1 - core) * (C // 2), 64), C // 2)],
+            part16.at[m, half(1 - core)],
             half_in.at[m],
             c_ss.at[m],
             c_rs.at[m],
@@ -467,53 +479,33 @@
         )
 
     def owned(m, e):
-        return lax.rem(e + xy - m * n_y, xy)
-
-    def copy_xy(m, to, sender, ss):
-        return pltpu.make_async_remote_copy(
-            chunks.at[m, lax.rem(owned(m, to), n_own)],
-            xy_in.at[m, sender],
-            xy_ss.at[m, ss],
-            xy_rs.at[m, sender],
-            device_id=at_spot(to, core),
-            device_id_type=MESH,
-        )
-
-    def copy_z(m, to, sender, ss):
-        return pltpu.make_async_remote_copy(
-            z_in.at[m, z],
-            z_in.at[m, sender],
-            z_ss.at[m, ss],
-            z_rs.at[m, sender],
-            device_id=at_z(to),
-            device_id_type=MESH,
-        )
-
-    def chunk(index):
-        return pl.ds(pl.multiple_of(index * chunk_rows, 16), chunk_rows)
-
-    def copy_final(m, index, ss, device):
-        return pltpu.make_async_remote_copy(
-            final.at[m, chunk(index)],
-            final.at[m, chunk(index)],
-            fin_ss.at[m, ss],
-            fin_rs.at[m, index],
-            device_id=device,
-            device_id_type=MESH,
-        )
-
-    def copy_spread(m, d):
-        device = at_spot(lax.rem(spot + d, xy), core)
-        return copy_final(m, core * n_own + lax.rem(owned(m, spot), n_own), d, device)
-
-    def copy_beside(m, i):
-        return copy_final(m, core * n_own + i, xy + i, sibling)
-
-    def far_first(k):
-        return n_z // 2 + (2 * lax.rem(k, 2) - 1) * (k // 2)
+        e = e - m * n_y
+        return jnp.where(e < 0, e + xy, e)
+
+    mine = [jnp.minimum(owned(m, spot), n_own - 1) for m in range(2)]
 
     def if_owner(m):
         return pl.when(owned(m, spot) < n_own)
+
+    def if_not_owner(m):
+        return pl.when(owned(m, spot) >= n_own)
+
+    def remote(source, target, ss, rs, device=sibling):
+        return pltpu.make_async_remote_copy(
+            source, target, ss, rs, device_id=device, device_id_type=MESH
+        )
+
+    def chunk(index, n=1):
+        return pl.ds(pl.multiple_of(index * chunk_rows, 16), n * chunk_rows)
+
+    def half(c):
+        return pl.ds(pl.multiple_of(c * (C // 2), 64), C // 2)
+
+    far_first = [d for i in range(n_z) for d in (n_z // 2 + i, n_z // 2 - i)]
+    far_first = [d for d in dict.fromkeys(far_first) if 0 < d < n_z]
+    z_steps = [far_first], [[8, 4, 12], [2, 1, 15]] if n_z == 16 else [far_first]
+    z_order = [z], [lax.div(z, 4), 4 + lax.rem(z, 4)] if n_z == 16 else [z]
+    z_slots = [(0, n_z)], [(0, 4), (4, 4)] if n_z == 16 else [(0, n_z)]
 
     def sum_start(m, total):
         part[m] = total
@@ -522,84 +514,91 @@
 
     def sum_xy(m):
         copy_core(m).wait_recv()
-        at = pl.ds(pl.multiple_of(core * (C // 2), 64), C // 2)
-        both = part[m, at, :] + half_in[m].astype(F32)
+        both = part[m, half(core), :] + half_in[m].astype(F32)
         chunks[m] = both.astype(BF16).reshape(n_own, chunk_rows, C)
-
-        def go(d):
-            to = lax.rem(spot + d, xy)
-
-            @if_owner_of(m, to)
+        for move in moves:
+            to, device = place(move)
+            k = owned(m, to)
+
+            @pl.when(k < n_own)
             def _():
-                copy_xy(m, to, spot, d).start()
-
-        each(xy, go)
-
-    def if_owner_of(m, e):
-        return pl.when(owned(m, e) < n_own)
+                source = chunks.at[m, jnp.minimum(k, n_own - 1)]
+                remote(source, xy_in.at[m, spot], xy_ss.at[m], xy_rs.at[m], device).start()
+
+    def z_send(m, i, value):
+        slot = z_order[m][i]
+        z_in[m, slot] = value.astype(BF16)
+        for d in z_steps[m][i]:
+            block = z_in.at[m, slot]
+            remote(block, block, z_ss.at[m, i], z_rs.at[m, i], at_z(d)).start()
+
+    def z_sum(m, i):
+        at, n = z_slots[m][i]
+        if n > 1:
+            several = z_in.at[m, at : at + n - 1]
+            remote(several, several, z_ss.at[m, i], z_rs.at[m, i]).wait_recv()
+        return jnp.sum(z_in[m, at : at + n].astype(F32), axis=0)
 
     def sum_z(m):
         @if_owner(m)
         def _():
-            xy_in[m, spot] = chunks[m, lax.rem(owned(m, spot), n_own)]
-            each(xy, lambda d: copy_xy(m, spot, lax.rem(spot + d, xy), d).wait_recv())
-            z_in[m, z] = jnp.sum(xy_in[m].astype(F32), axis=0).astype(BF16)
-
-            def go(k):
-                d = far_first(k)
-                copy_z(m, lax.rem(z + d, n_z), z, d).start()
-
-            each(n_z, go)
+            xy_in[m, spot] = chunks[m, mine[m]]
+            several = xy_in.at[m, 0 : xy - 1]
+            remote(several, several, xy_ss.at[m], xy_rs.at[m]).wait_recv()
+            z_send(m, 0, jnp.sum(xy_in[m].astype(F32), axis=0))
+
+    def sum_z_again(m):
+        if len(z_steps[m]) > 1:
+
+            @if_owner(m)
+            def _():
+                z_send(m, 1, z_sum(m, 0))
 
     def sum_back(m):
         @if_owner(m)
         def _():
-            each(n_z, lambda d: copy_z(m, z, lax.rem(z + d, n_z), d).wait_recv())
-            index = core * n_own + lax.rem(owned(m, spot), n_own)
-            final[m, chunk(index), :] = jnp.sum(z_in[m].astype(F32), axis=0).astype(BF16)
-            each(xy, lambda d: copy_spread(m, d).start())
+            block = final.at[m, chunk(core * n_own + mine[m])]
+            final[m, chunk(core * n_own + mine[m]), :] = z_sum(m, len(z_steps[m]) - 1).astype(BF16)
+            for move in moves:
+                remote(block, block, fin_ss.at[m], fin_rs.at[m], place(move)[1]).start()
 
     def sum_share(m):
-        def take(i, carry):
-            @pl.when(owned(m, spot) != i)
-            def _():
-                copy_final(m, core * n_own + i, 0, sibling).wait_recv()
-
-            copy_beside(m, i).start()
-            return carry
-
-        lax.fori_loop(0, n_own, take, 0)
+        def wait(n):
+            several = final.at[m, 0 : n * chunk_rows]
+            remote(several, several, fin_ss.at[m], fin_rs.at[m]).wait_recv()
+
+        if_owner(m)(lambda: wait(n_own - 1))
+        if_not_owner(m)(lambda: wait(n_own))
+        block = final.at[m, half(core)]
+        remote(block, block, half_ss.at[m], half_rs.at[m]).start()
 
     def sum_end(m):
-        def take(i, carry):
-            copy_final(m, (1 - core) * n_own + i, 0, sibling).wait_recv()
-            return carry
-
-        lax.fori_loop(0, n_own, take, 0)
+        block = final.at[m, half(core)]
+        remote(block, block, half_ss.at[m], half_rs.at[m]).wait_recv()
         results[m].start()
 
     def sum_sent(m):
         copy_core(m).wait_send()
-
-        def sent(d):
-            to = lax.rem(spot + d, xy)
-
-            @if_owner_of(m, to)
-            def _():
-                copy_xy(m, to, spot, d).wait_send()
-
-        each(xy, sent)
+        block = final.at[m, half(core)]
+        remote(block, block, half_ss.at[m], half_rs.at[m]).wait_send()
+
+        def wait(n):
+            several = chunks.at[m, 0:n]
+            remote(several, several, xy_ss.at[m], xy_rs.at[m]).wait_send()
+
+        @if_not_owner(m)
+        def _():
+            wait(n_own)
 
         @if_owner(m)
         def _():
-            each(n_z, lambda d: copy_z(m, lax.rem(z + d, n_z), z, d).wait_send())
-            each(xy, lambda d: copy_spread(m, d).wait_send())
-
-        def passed(i, carry):
-            copy_beside(m, i).wait_send()
-            return carry
-
-        lax.fori_loop(0, n_own, passed, 0)
+            wait(n_own - 1)
+            several = xy_in.at[m, 0 : xy - 1]
+            remote(several, several, fin_ss.at[m], fin_rs.at[m]).wait_send()
+            for i, (at, n) in enumerate(z_slots[m]):
+                if n > 1:
+                    several = z_in.at[m, at : at + n - 1]
+                    remote(several, several, z_ss.at[m, i], z_rs.at[m, i]).wait_send()
 
     n1 = norm(xf[...], xhat_p, rstd_p)
     loads["tab_p"].wait()
@@ -686,6 +685,7 @@
     for i in range(WLAT * WLON):
         field_out[i] = s2f[2 * i : 2 * i + 2, :].astype(BF16)
     results[2].start()
+    sum_z_again(1)
     sum_back(1)
     sum_back(0)
     for copies in (halo_cot, halo_h1, halo_o1, halo_g1, halo_out, first[1:], beside):

time: 71.2 us -> 65.7 us (0.923)
  Pallas kernels: 70.4 us -> 64.9 us
    pallas_call x1, Pallas kernels: 68.5 us -> 63 us  [body(): pl.pallas_call(functools.partial(kernel, sizes, plan, names), out_shape=(...]
where the time goes in v4:
time: 65.7 us; the launch traced here: 65.6 us
  Pallas kernels  64.9 us (99%)
    pallas_call x1, Pallas kernels, body(): pl.pallas_call(functools.partial(kernel, sizes, plan, names), out_shape=(...  63 us
    pallas_call x1, Pallas kernels, body(): pl.pallas_call(store, out_shape=tuple((jax.ShapeDtypeStruct(x.shape, x.dt...  1.96 us

profile of v4, /device:TPU:1, one launch (start us, length us, event | category | flops | bytes accessed | tf_op | source)
XLA Modules:
  0.0 65.6 jit_solution(4868998723685201963)
XLA Ops:
  0.6 63.0 %shard_map.138 = (bf16[72,2,384]{2,1,0:T(2,128)(2,1)}, bf16[72,2,384]{2,1,0:T(2,128)(2,1)}, bf16[384,384]{1,0:T(8,128)(2,1)}, bf16[384,384]{1,0:T(8,128)(2,1)}) custom-call(bf16[72,2,384]{2,1,0:T(2,128)(2,1)} %bitcast.20, bf16[72,2,384]{2,1,0:T(2,128)(2,1)} %bitcast.21, bf16[576,384]{1,0:T(8,128)(2,1)} %bitcast.16, bf16[576,384]{1,0:T(8,128)(2,1)} %bitcast.17, ...), custom_call_target="tpu_custom_call" | custom-call | tf_op jit(solution)/shard_map/pallas_call | solution.py:745
  63.6 2.0 %shard_map.139 = (bf16[72,2,384]{2,1,0:T(2,128)(2,1)}, bf16[72,2,384]{2,1,0:T(2,128)(2,1)}, bf16[384,384]{1,0:T(8,128)(2,1)}, bf16[384,384]{1,0:T(8,128)(2,1)}) custom-call(bf16[72,2,384]{2,1,0:T(2,128)(2,1)} %get-tuple-element.12.refs_0_, bf16[72,2,384]{2,1,0:T(2,128)(2,1)} %get-tuple-element.13.refs_1_, bf16[384,384]{1,0:T(8,128)(2,1)} %get-tuple-element.14.refs_2_, ...), custom_call_target="tpu_custom_call" | custom-call | tf_op jit(solution)/shard_map/pallas_call | solution.py:757

commit v5 on v4

--- a/solution.py
+++ b/solution.py
@@ -103,21 +103,21 @@
         probs_s=full_bias,
         ot_p=heads_t,
         ot_s=heads_t,
-        ot_r=heads_t,
         dqkv=qkv,
         dqt=pltpu.VMEM((C, TOKENS), F32),
         bias_p=full_bias,
         bias_s=full_bias,
         tabf=pltpu.VMEM((16, 6400), F32),
-        spread=pltpu.VMEM((2, TOKENS * 16, 128), F32),
+        spread_p=pltpu.VMEM((2, TOKENS * 16, 128), F32),
+        spread_s=pltpu.VMEM((2, TOKENS * 16, 128), F32),
         send=pltpu.VMEM((5, 4, QUAD, C), BF16),
         recv=pltpu.VMEM((5, 4, QUAD, C), BF16),
         halo_ss=dma((5, 4)),
         halo_rs=dma((5, 4)),
-        w_ss=dma((2,)),
-        w_rs=dma((2,)),
-        f_ss=dma((2,)),
-        f_rs=dma((2,)),
+        w_ss=dma((4,)),
+        w_rs=dma((4,)),
+        f_ss=dma((4,)),
+        f_rs=dma((4,)),
         part=pltpu.VMEM((2, C, C), F32),
         part16=pltpu.VMEM((2, C, C), BF16),
         half_in=pltpu.VMEM((2, C // 2, C), BF16),
@@ -172,13 +172,13 @@
     probs_s,
     ot_p,
     ot_s,
-    ot_r,
     dqkv,
     dqt,
     bias_p,
     bias_s,
     tabf,
-    spread,
+    spread_p,
+    spread_s,
     send,
     recv,
     halo_ss,
@@ -262,7 +262,7 @@
     y_up, y_down = near(2, 0), near(-2, 0)
     barrier = pltpu.get_barrier_semaphore()
     around = [across, sibling, beside_x, y_up, y_down, along_z(1), along_z(-1)]
-    around += [near(a, b) for a, b in ((1, 0), (-1, 0), (0, 1), (0, -1), (1, 1), (-1, -1))]
+    around += [near(a, b) for a, b in ((1, 0), (-1, 0), (0, 1), (0, -1))]
     for device in around:
         greet(barrier, device)
 
@@ -271,9 +271,12 @@
             greet(roll.at[i], device)
         for d in (2**i, -(2**i)):
             greet(roll.at[i], along_z(d))
+        if i == 0:
+            greet(roll.at[i], near(1, 0))
+            greet(roll.at[i], near(-1, 0))
 
     def told(i):
-        pl.semaphore_wait(roll.at[i], 7)
+        pl.semaphore_wait(roll.at[i], 9 if i == 0 else 7)
 
     results = [
         pltpu.make_async_copy(a, b, out_sem.at[i])
@@ -296,27 +299,32 @@
     )
     pl.semaphore_wait(barrier, len(around))
 
-    rows = pl.ds(pl.multiple_of(core * 288, 32), 288)
-
-    def weights_across(half, full, i):
+    def piece(i, n):
+        size = 288 // n
+        return pl.ds(pl.multiple_of(core * 288 + i * size, 16), size)
+
+    def weights_across(source, full, at, i):
         return pltpu.make_async_remote_copy(
-            half.at[rows],
-            full.at[dp, rows],
+            source.at[at],
+            full.at[dp, at],
             w_ss.at[i],
             w_rs.at[i],
             device_id=across,
             device_id_type=MESH,
         )
 
-    def weights_beside(full, i):
-        part = full.at[1 - dp, rows]
+    def weights_beside(full, at, i):
+        part = full.at[1 - dp, at]
         return pltpu.make_async_remote_copy(
             part, part, f_ss.at[i], f_rs.at[i], device_id=sibling, device_id_type=MESH
         )
 
-    first = [weights_across(wp_half, wp, 0), weights_across(ws_half, ws, 1)]
-    first[0].start()
-    beside = [weights_beside(wp, 0), weights_beside(ws, 1)]
+    places = [(wp_half, wp, piece(i, 3)) for i in range(3)] + [(ws_half, ws, piece(0, 1))]
+    first = [weights_across(*place, i) for i, place in enumerate(places)]
+    beside = [weights_beside(*place[1:], i) for i, place in enumerate(places)]
+    for copy in first[:3]:
+        copy.start()
+    tell(0)
 
     def halo(i, by):
         kept = 3 if by < 0 else 0
@@ -356,8 +364,6 @@
             at = ((h // 6) * 2 + w // 3) * QUAD + ((h % 6) * 3 + w % 3) * 2
             quads[at : at + 2, :] = cot[h * WLON + w].astype(F32)
     send[0] = quads[...].astype(BF16).reshape(4, QUAD, C)
-    halo_cot = halo(0, -1)
-    tell(0)
 
     loads["field"].wait()
     for i in range(WLAT * WLON):
@@ -374,7 +380,7 @@
 
     lane256 = lax.broadcasted_iota(jnp.int32, (16, 256), 1)
 
-    def expand(tab, bias, hide):
+    def align(tab, spread):
         tabf[...] = jnp.zeros_like(tabf)
         tabf[0:HEADS, 0 : 4 * WLAT * CHUNK] = tab[...].astype(F32)
 
@@ -399,6 +405,8 @@
             return carry
 
         lax.fori_loop(0, WLAT, row, 0)
+
+    def expand(spread, bias, hide):
         for head in range(HEADS):
             lanes = [spread[half, pl.ds(head, TOKENS, stride=16), :] for half in range(2)]
             table = jnp.concatenate(lanes, axis=1).astype(BF16)
@@ -503,9 +511,9 @@
 
     far_first = [d for i in range(n_z) for d in (n_z // 2 + i, n_z // 2 - i)]
     far_first = [d for d in dict.fromkeys(far_first) if 0 < d < n_z]
-    z_steps = [far_first], [[8, 4, 12], [2, 1, 15]] if n_z == 16 else [far_first]
-    z_order = [z], [lax.div(z, 4), 4 + lax.rem(z, 4)] if n_z == 16 else [z]
-    z_slots = [(0, n_z)], [(0, 4), (4, 4)] if n_z == 16 else [(0, n_z)]
+    z_steps = [[8, 4, 12], [2, 1, 15]] if n_z == 16 else [far_first]
+    z_order = [lax.div(z, 4), 4 + lax.rem(z, 4)] if n_z == 16 else [z]
+    z_slots = [(0, 4), (4, 4)] if n_z == 16 else [(0, n_z)]
 
     def sum_start(m, total):
         part[m] = total
@@ -526,14 +534,14 @@
                 remote(source, xy_in.at[m, spot], xy_ss.at[m], xy_rs.at[m], device).start()
 
     def z_send(m, i, value):
-        slot = z_order[m][i]
+        slot = z_order[i]
         z_in[m, slot] = value.astype(BF16)
-        for d in z_steps[m][i]:
+        for d in z_steps[i]:
             block = z_in.at[m, slot]
             remote(block, block, z_ss.at[m, i], z_rs.at[m, i], at_z(d)).start()
 
     def z_sum(m, i):
-        at, n = z_slots[m][i]
+        at, n = z_slots[i]
         if n > 1:
             several = z_in.at[m, at : at + n - 1]
             remote(several, several, z_ss.at[m, i], z_rs.at[m, i]).wait_recv()
@@ -548,7 +556,7 @@
             z_send(m, 0, jnp.sum(xy_in[m].astype(F32), axis=0))
 
     def sum_z_again(m):
-        if len(z_steps[m]) > 1:
+        if len(z_steps) > 1:
 
             @if_owner(m)
             def _():
@@ -558,7 +566,7 @@
         @if_owner(m)
         def _():
             block = final.at[m, chunk(core * n_own + mine[m])]
-            final[m, chunk(core * n_own + mine[m]), :] = z_sum(m, len(z_steps[m]) - 1).astype(BF16)
+            final[m, chunk(core * n_own + mine[m]), :] = z_sum(m, len(z_steps) - 1).astype(BF16)
             for move in moves:
                 remote(block, block, fin_ss.at[m], fin_rs.at[m], place(move)[1]).start()
 
@@ -595,23 +603,35 @@
             wait(n_own - 1)
             several = xy_in.at[m, 0 : xy - 1]
             remote(several, several, fin_ss.at[m], fin_rs.at[m]).wait_send()
-            for i, (at, n) in enumerate(z_slots[m]):
+            for i, (at, n) in enumerate(z_slots):
                 if n > 1:
                     several = z_in.at[m, at : at + n - 1]
                     remote(several, several, z_ss.at[m, i], z_rs.at[m, i]).wait_send()
 
     n1 = norm(xf[...], xhat_p, rstd_p)
     loads["tab_p"].wait()
+    align(tab_p, spread_p)
     loads["pick"].wait()
-    expand(tab_p, bias_p, None)
-    first[0].wait_send()
-    first[1].start()
+    expand(spread_p, bias_p, None)
     told(0)
     tell(1)
-    loads["wp_half"].wait()
+    halo_cot = halo(0, -1)
     first[0].wait_recv()
     beside[0].start()
-    beside[0].wait_recv()
+    loads["tab_s"].wait()
+    align(tab_s, spread_s)
+    first[1].wait_recv()
+    beside[1].start()
+    for copy in first[:3]:
+        copy.wait_send()
+    first[3].start()
+    first[2].wait_recv()
+    beside[2].start()
+    loads["wp_half"].wait()
+    for copy in beside[:3]:
+        copy.wait_recv()
+    told(1)
+    tell(2)
     project(n1, wp, qkv_p, kvt_p)
     for g in range(GROUPS):
         p = softmax(g, qkv_p, bias_p)
@@ -622,26 +642,23 @@
     o1 = heads(ot_p)
     to_quads(1, output(xf[...], o1, proj_p))
     halo_h1 = halo(1, -1)
-    to_quads(4, o1)
-    halo_o1 = halo(4, -1)
-    told(1)
-    tell(2)
 
     key = lax.broadcasted_iota(jnp.int32, (TOKENS, TOKENS), 0)
     query = lax.broadcasted_iota(jnp.int32, (TOKENS, TOKENS), 1)
     edge = jnp.where(lat == n_lat - 1, TOKENS // 2, TOKENS)
     same = ((key & 1) == (query & 1)) & ((key >= edge) == (query >= edge))
-    loads["tab_s"].wait()
-    expand(tab_s, bias_s, jnp.where(same, 0.0, -1e30))
-    loads["ws_half"].wait()
-    first[1].wait_recv()
-    beside[1].start()
+    to_quads(4, o1)
+    halo_o1 = halo(4, -1)
+    expand(spread_s, bias_s, jnp.where(same, 0.0, -1e30))
+    first[3].wait_recv()
+    beside[3].start()
     loads["gather"].wait()
     dy2 = arrived(0, halo_cot)
     dy2f[...] = dy2
     loads["proj_s"].wait()
     do2 = nt(dy2.astype(BF16), proj_s[...]).astype(BF16)
-    beside[1].wait_recv()
+    loads["ws_half"].wait()
+    beside[3].wait_recv()
     told(2)
 
     s2 = arrived(1, halo_h1)
@@ -656,11 +673,10 @@
     for g in range(GROUPS):
         p = probs_s[g * PER : (g + 1) * PER]
         grads(g, p, p.astype(BF16), do2, qkv_s, kvt_s)
-        if g == 0:
-            sum_xy(1)
-            ot_r[...] = arrived(4, halo_o1).T.astype(BF16)
+    sum_xy(1)
     ds2 = input_grad(dy2f[...], ws, xhat_s, rstd_s)
-    sum_start(0, nn(ot_r[...], ds2))
+    ot_r = arrived(4, halo_o1).T.astype(BF16)
+    sum_start(0, nn(ot_r, ds2))
     to_quads(2, ds2)
     halo_g1 = halo(2, 1)
 
@@ -686,9 +702,10 @@
         field_out[i] = s2f[2 * i : 2 * i + 2, :].astype(BF16)
     results[2].start()
     sum_z_again(1)
+    sum_z_again(0)
     sum_back(1)
     sum_back(0)
-    for copies in (halo_cot, halo_h1, halo_o1, halo_g1, halo_out, first[1:], beside):
+    for copies in (halo_cot, halo_h1, halo_o1, halo_g1, halo_out, first[3:], beside):
         for copy in copies:
             copy.wait_send()
     sum_share(1)

time: 65.7 us -> 61.2 us (0.932)
  Pallas kernels: 64.9 us -> 60.4 us
    pallas_call x1, Pallas kernels: 63 us -> 58.5 us  [body(): pl.pallas_call(functools.partial(kernel, sizes, plan, names), out_shape=(...]
where the time goes in v5:
time: 61.2 us; the launch traced here: 61.1 us
  Pallas kernels  60.4 us (99%)
  between operations  0.64 us (1%)
    pallas_call x1, Pallas kernels, body(): pl.pallas_call(functools.partial(kernel, sizes, plan, names), out_shape=(...  58.5 us
    pallas_call x1, Pallas kernels, body(): pl.pallas_call(store, out_shape=tuple((jax.ShapeDtypeStruct(x.shape, x.dt...  1.96 us

profile of v5, /device:TPU:1, one launch (start us, length us, event | category | flops | bytes accessed | tf_op | source)
XLA Modules:
  0.0 61.1 jit_solution(7917498532584012854)
XLA Ops:
  0.6 58.5 %shard_map.138 = (bf16[72,2,384]{2,1,0:T(2,128)(2,1)}, bf16[72,2,384]{2,1,0:T(2,128)(2,1)}, bf16[384,384]{1,0:T(8,128)(2,1)}, bf16[384,384]{1,0:T(8,128)(2,1)}) custom-call(bf16[72,2,384]{2,1,0:T(2,128)(2,1)} %bitcast.20, bf16[72,2,384]{2,1,0:T(2,128)(2,1)} %bitcast.21, bf16[576,384]{1,0:T(8,128)(2,1)} %bitcast.16, bf16[576,384]{1,0:T(8,128)(2,1)} %bitcast.17, ...), custom_call_target="tpu_custom_call" | custom-call | tf_op jit(solution)/shard_map/pallas_call | solution.py:762
  59.1 2.0 %shard_map.139 = (bf16[72,2,384]{2,1,0:T(2,128)(2,1)}, bf16[72,2,384]{2,1,0:T(2,128)(2,1)}, bf16[384,384]{1,0:T(8,128)(2,1)}, bf16[384,384]{1,0:T(8,128)(2,1)}) custom-call(bf16[72,2,384]{2,1,0:T(2,128)(2,1)} %get-tuple-element.12.refs_0_, bf16[72,2,384]{2,1,0:T(2,128)(2,1)} %get-tuple-element.13.refs_1_, bf16[384,384]{1,0:T(8,128)(2,1)} %get-tuple-element.14.refs_2_, ...), custom_call_target="tpu_custom_call" | custom-call | tf_op jit(solution)/shard_map/pallas_call | solution.py:774

commit v6 on v5

--- a/solution.py
+++ b/solution.py
@@ -380,9 +380,10 @@
 
     lane256 = lax.broadcasted_iota(jnp.int32, (16, 256), 1)
 
-    def align(tab, spread):
-        tabf[...] = jnp.zeros_like(tabf)
-        tabf[0:HEADS, 0 : 4 * WLAT * CHUNK] = tab[...].astype(F32)
+    def align(tab, spread, start, stop):
+        if start == 0:
+            tabf[...] = jnp.zeros_like(tabf)
+            tabf[0:HEADS, 0 : 4 * WLAT * CHUNK] = tab[...].astype(F32)
 
         def row(h, carry):
             for za in range(LEV):
@@ -404,7 +405,7 @@
                     spread[1, pl.ds(at, 16), :] = both[:, 128:]
             return carry
 
-        lax.fori_loop(0, WLAT, row, 0)
+        lax.fori_loop(start, stop, row, 0)
 
     def expand(spread, bias, hide):
         for head in range(HEADS):
@@ -610,23 +611,20 @@
 
     n1 = norm(xf[...], xhat_p, rstd_p)
     loads["tab_p"].wait()
-    align(tab_p, spread_p)
+    align(tab_p, spread_p, 0, WLAT)
     loads["pick"].wait()
     expand(spread_p, bias_p, None)
     told(0)
     tell(1)
     halo_cot = halo(0, -1)
-    first[0].wait_recv()
-    beside[0].start()
     loads["tab_s"].wait()
-    align(tab_s, spread_s)
-    first[1].wait_recv()
-    beside[1].start()
+    align(tab_s, spread_s, 0, 6)
+    for arriving, passed_on in zip(first[:3], beside[:3]):
+        arriving.wait_recv()
+        passed_on.start()
     for copy in first[:3]:
         copy.wait_send()
     first[3].start()
-    first[2].wait_recv()
-    beside[2].start()
     loads["wp_half"].wait()
     for copy in beside[:3]:
         copy.wait_recv()
@@ -643,20 +641,21 @@
     to_quads(1, output(xf[...], o1, proj_p))
     halo_h1 = halo(1, -1)
 
+    loads["gather"].wait()
+    dy2 = arrived(0, halo_cot)
+    dy2f[...] = dy2
+    loads["proj_s"].wait()
+    do2 = nt(dy2.astype(BF16), proj_s[...]).astype(BF16)
     key = lax.broadcasted_iota(jnp.int32, (TOKENS, TOKENS), 0)
     query = lax.broadcasted_iota(jnp.int32, (TOKENS, TOKENS), 1)
     edge = jnp.where(lat == n_lat - 1, TOKENS // 2, TOKENS)
     same = ((key & 1) == (query & 1)) & ((key >= edge) == (query >= edge))
     to_quads(4, o1)
     halo_o1 = halo(4, -1)
-    expand(spread_s, bias_s, jnp.where(same, 0.0, -1e30))
+    align(tab_s, spread_s, 6, WLAT)
     first[3].wait_recv()
     beside[3].start()
-    loads["gather"].wait()
-    dy2 = arrived(0, halo_cot)
-    dy2f[...] = dy2
-    loads["proj_s"].wait()
-    do2 = nt(dy2.astype(BF16), proj_s[...]).astype(BF16)
+    expand(spread_s, bias_s, jnp.where(same, 0.0, -1e30))
     loads["ws_half"].wait()
     beside[3].wait_recv()
     told(2)

time: 61.2 us -> 60.6 us (level)
    pallas_call x1, Pallas kernels: 58.5 us -> 57.8 us  [body(): pl.pallas_call(functools.partial(kernel, sizes, plan, names), out_shape=(...]
where the time goes in v6:
time: 60.6 us; the launch traced here: 60.4 us
  Pallas kernels  59.8 us (99%)
  between operations  0.64 us (1%)
    pallas_call x1, Pallas kernels, body(): pl.pallas_call(functools.partial(kernel, sizes, plan, names), out_shape=(...  57.8 us
    pallas_call x1, Pallas kernels, body(): pl.pallas_call(store, out_shape=tuple((jax.ShapeDtypeStruct(x.shape, x.dt...  1.96 us

profile of v6, /device:TPU:1, one launch (start us, length us, event | category | flops | bytes accessed | tf_op | source)
XLA Modules:
  0.0 60.4 jit_solution(18093496099257489755)
XLA Ops:
  0.6 57.8 %shard_map.138 = (bf16[72,2,384]{2,1,0:T(2,128)(2,1)}, bf16[72,2,384]{2,1,0:T(2,128)(2,1)}, bf16[384,384]{1,0:T(8,128)(2,1)}, bf16[384,384]{1,0:T(8,128)(2,1)}) custom-call(bf16[72,2,384]{2,1,0:T(2,128)(2,1)} %bitcast.20, bf16[72,2,384]{2,1,0:T(2,128)(2,1)} %bitcast.21, bf16[576,384]{1,0:T(8,128)(2,1)} %bitcast.16, bf16[576,384]{1,0:T(8,128)(2,1)} %bitcast.17, ...), custom_call_target="tpu_custom_call" | custom-call | tf_op jit(solution)/shard_map/pallas_call | solution.py:761
  58.5 2.0 %shard_map.139 = (bf16[72,2,384]{2,1,0:T(2,128)(2,1)}, bf16[72,2,384]{2,1,0:T(2,128)(2,1)}, bf16[384,384]{1,0:T(8,128)(2,1)}, bf16[384,384]{1,0:T(8,128)(2,1)}) custom-call(bf16[72,2,384]{2,1,0:T(2,128)(2,1)} %get-tuple-element.12.refs_0_, bf16[72,2,384]{2,1,0:T(2,128)(2,1)} %get-tuple-element.13.refs_1_, bf16[384,384]{1,0:T(8,128)(2,1)} %get-tuple-element.14.refs_2_, ...), custom_call_target="tpu_custom_call" | custom-call | tf_op jit(solution)/shard_map/pallas_call | solution.py:773

commit v7 on v6

--- a/solution.py
+++ b/solution.py
@@ -704,13 +704,13 @@
     sum_z_again(0)
     sum_back(1)
     sum_back(0)
-    for copies in (halo_cot, halo_h1, halo_o1, halo_g1, halo_out, first[3:], beside):
-        for copy in copies:
-            copy.wait_send()
     sum_share(1)
     sum_share(0)
     sum_end(1)
     sum_end(0)
+    for copies in (halo_cot, halo_h1, halo_o1, halo_g1, halo_out, first[3:], beside):
+        for copy in copies:
+            copy.wait_send()
     sum_sent(1)
     sum_sent(0)
     for copy in results:

time: 60.6 us -> 60.6 us (level)
  no operation moved by 1% of the time
where the time goes in v7:
time: 60.6 us; the launch traced here: 60.4 us
  Pallas kernels  59.8 us (99%)
  between operations  0.64 us (1%)
    pallas_call x1, Pallas kernels, body(): pl.pallas_call(functools.partial(kernel, sizes, plan, names), out_shape=(...  57.8 us
    pallas_call x1, Pallas kernels, body(): pl.pallas_call(store, out_shape=tuple((jax.ShapeDtypeStruct(x.shape, x.dt...  1.96 us

profile of v7, /device:TPU:1, one launch (start us, length us, event | category | flops | bytes accessed | tf_op | source)
XLA Modules:
  0.0 60.4 jit_solution(13643189155531560958)
XLA Ops:
  0.6 57.8 %shard_map.138 = (bf16[72,2,384]{2,1,0:T(2,128)(2,1)}, bf16[72,2,384]{2,1,0:T(2,128)(2,1)}, bf16[384,384]{1,0:T(8,128)(2,1)}, bf16[384,384]{1,0:T(8,128)(2,1)}) custom-call(bf16[72,2,384]{2,1,0:T(2,128)(2,1)} %bitcast.20, bf16[72,2,384]{2,1,0:T(2,128)(2,1)} %bitcast.21, bf16[576,384]{1,0:T(8,128)(2,1)} %bitcast.16, bf16[576,384]{1,0:T(8,128)(2,1)} %bitcast.17, ...), custom_call_target="tpu_custom_call" | custom-call | tf_op jit(solution)/shard_map/pallas_call | solution.py:761
  58.5 2.0 %shard_map.139 = (bf16[72,2,384]{2,1,0:T(2,128)(2,1)}, bf16[72,2,384]{2,1,0:T(2,128)(2,1)}, bf16[384,384]{1,0:T(8,128)(2,1)}, bf16[384,384]{1,0:T(8,128)(2,1)}) custom-call(bf16[72,2,384]{2,1,0:T(2,128)(2,1)} %get-tuple-element.12.refs_0_, bf16[72,2,384]{2,1,0:T(2,128)(2,1)} %get-tuple-element.13.refs_1_, bf16[384,384]{1,0:T(8,128)(2,1)} %get-tuple-element.14.refs_2_, ...), custom_call_target="tpu_custom_call" | custom-call | tf_op jit(solution)/shard_map/pallas_call | solution.py:773

commit v8 on v7

--- a/solution.py
+++ b/solution.py
@@ -118,8 +118,9 @@
         w_rs=dma((4,)),
         f_ss=dma((4,)),
         f_rs=dma((4,)),
-        part=pltpu.VMEM((2, C, C), F32),
-        part16=pltpu.VMEM((2, C, C), BF16),
+        left=pltpu.VMEM((2, C, TOKENS), BF16),
+        part=pltpu.VMEM((2, C // 2, C), F32),
+        part16=pltpu.VMEM((2, C // 2, C), BF16),
         half_in=pltpu.VMEM((2, C // 2, C), BF16),
         chunks=pltpu.VMEM((2, C // 2 // rows, rows, C), BF16),
         xy_in=pltpu.VMEM((2, xy, rows, C), BF16),
@@ -187,6 +188,7 @@
     w_rs,
     f_ss,
     f_rs,
+    left,
     part,
     part16,
     half_in,
@@ -479,7 +481,7 @@
 
     def copy_core(m):
         return pltpu.make_async_remote_copy(
-            part16.at[m, half(1 - core)],
+            part16.at[m],
             half_in.at[m],
             c_ss.at[m],
             c_rs.at[m],
@@ -516,14 +518,15 @@
     z_order = [lax.div(z, 4), 4 + lax.rem(z, 4)] if n_z == 16 else [z]
     z_slots = [(0, 4), (4, 4)] if n_z == 16 else [(0, n_z)]
 
-    def sum_start(m, total):
-        part[m] = total
-        part16[m] = total.astype(BF16)
+    def sum_start(m, ot, dy):
+        left[m] = ot
+        part16[m] = nn(left[m, half(1 - core), :], dy).astype(BF16)
         copy_core(m).start()
+        part[m] = nn(left[m, half(core), :], dy)
 
     def sum_xy(m):
         copy_core(m).wait_recv()
-        both = part[m, half(core), :] + half_in[m].astype(F32)
+        both = part[m] + half_in[m].astype(F32)
         chunks[m] = both.astype(BF16).reshape(n_own, chunk_rows, C)
         for move in moves:
             to, device = place(move)
@@ -668,14 +671,14 @@
         p = softmax(g, qkv_s, bias_s)
         probs_s[g * PER : (g + 1) * PER] = p
         values(g, p.astype(BF16), kvt_s, ot_s)
-    sum_start(1, nn(ot_s[...], dy2f[...].astype(BF16)))
+    sum_start(1, ot_s[...], dy2f[...].astype(BF16))
     for g in range(GROUPS):
         p = probs_s[g * PER : (g + 1) * PER]
         grads(g, p, p.astype(BF16), do2, qkv_s, kvt_s)
     sum_xy(1)
     ds2 = input_grad(dy2f[...], ws, xhat_s, rstd_s)
     ot_r = arrived(4, halo_o1).T.astype(BF16)
-    sum_start(0, nn(ot_r, ds2))
+    sum_start(0, ot_r, ds2)
     to_quads(2, ds2)
     halo_g1 = halo(2, 1)
 

time: 60.6 us -> 61 us (level)
  no operation moved by 1% of the time
where the time goes in v8:
time: 61 us; the launch traced here: 60.9 us
  Pallas kernels  60.3 us (99%)
  between operations  0.64 us (1%)
    pallas_call x1, Pallas kernels, body(): pl.pallas_call(functools.partial(kernel, sizes, plan, names), out_shape=(...  58.3 us
    pallas_call x1, Pallas kernels, body(): pl.pallas_call(store, out_shape=tuple((jax.ShapeDtypeStruct(x.shape, x.dt...  1.96 us

profile of v8, /device:TPU:1, one launch (start us, length us, event | category | flops | bytes accessed | tf_op | source)
XLA Modules:
  0.0 60.9 jit_solution(3285675554293617937)
XLA Ops:
  0.6 58.3 %shard_map.138 = (bf16[72,2,384]{2,1,0:T(2,128)(2,1)}, bf16[72,2,384]{2,1,0:T(2,128)(2,1)}, bf16[384,384]{1,0:T(8,128)(2,1)}, bf16[384,384]{1,0:T(8,128)(2,1)}) custom-call(bf16[72,2,384]{2,1,0:T(2,128)(2,1)} %bitcast.20, bf16[72,2,384]{2,1,0:T(2,128)(2,1)} %bitcast.21, bf16[576,384]{1,0:T(8,128)(2,1)} %bitcast.16, bf16[576,384]{1,0:T(8,128)(2,1)} %bitcast.17, ...), custom_call_target="tpu_custom_call" | custom-call | tf_op jit(solution)/shard_map/pallas_call | solution.py:764
  58.9 2.0 %shard_map.139 = (bf16[72,2,384]{2,1,0:T(2,128)(2,1)}, bf16[72,2,384]{2,1,0:T(2,128)(2,1)}, bf16[384,384]{1,0:T(8,128)(2,1)}, bf16[384,384]{1,0:T(8,128)(2,1)}) custom-call(bf16[72,2,384]{2,1,0:T(2,128)(2,1)} %get-tuple-element.12.refs_0_, bf16[72,2,384]{2,1,0:T(2,128)(2,1)} %get-tuple-element.13.refs_1_, bf16[384,384]{1,0:T(8,128)(2,1)} %get-tuple-element.14.refs_2_, ...), custom_call_target="tpu_custom_call" | custom-call | tf_op jit(solution)/shard_map/pallas_call | solution.py:776
